TPU v7x, 32 devices: a whole 2x2x4 slice. The times are simulated.
32 devices in a mesh: dp: 8 (over z, x), seq: 4 (over y, core).
Axes of the slice: x: 2, y: 2, z: 4, core: 2. Of those that a mesh axis runs over, the one named last changes fastest.
Arguments:
- tokens: bfloat16 [16, 1024, 1024], P(None, 'seq', 'dp'), may hold values from -6 to 6
- cotangent: bfloat16 [16, 1024, 1024], P('dp', 'seq'), may hold values from -6 to 6
- seq_lengths: int32 [16, 4], replicated, may hold values from 0 to 1024, as said below
- deal_order: int32 [16], replicated, may hold values from 0 to 15, as said below
- in_gain: bfloat16 [1024], P('dp'), may hold values from 0.5 to 1.5
- in_proj: bfloat16 [1024, 4096], P('dp'), may hold values from -0.1875 to 0.1875
- dt_proj: bfloat16 [1024, 24], P('dp'), may hold values from -0.1875 to 0.1875
- dt_bias: float32 [24], replicated, may hold values from -7 to -3
- a_log: float32 [24], replicated, may hold values from 0 to 2.5
- d_skip: float32 [24], replicated, may hold values from 0.5 to 2
- ssm_out: bfloat16 [1536, 1024], P('dp'), may hold values from -0.15625 to 0.15625
- attn_out: bfloat16 [512, 1024], P('dp'), may hold values from -1 to 1
- ffn_gain: bfloat16 [1024], P('dp'), may hold values from 0.5 to 1.5
- gate_up: bfloat16 [1024, 4096], P('dp'), may hold values from -0.1875 to 0.1875
- down_proj: bfloat16 [2048, 1024], P('dp'), may hold values from -0.125 to 0.125
Outputs:
- output: bfloat16 [16, 1024, 1024], P('dp', 'seq')
- grad_tokens: bfloat16 [16, 1024, 1024], P(None, 'seq', 'dp')
- grad_in_gain: float32 [1024], P('dp')
- grad_in_proj: float32 [1024, 4096], P('dp')
- grad_dt_proj: float32 [1024, 24], P('dp')
- grad_dt_bias: float32 [24], replicated
- grad_a_log: float32 [24], replicated
- grad_d_skip: float32 [24], replicated
- grad_ssm_out: float32 [1536, 1024], P('dp')
- grad_attn_out: float32 [512, 1024], P('dp')
- grad_ffn_gain: float32 [1024], P('dp')
- grad_gate_up: float32 [1024, 4096], P('dp')
- grad_down_proj: float32 [2048, 1024], P('dp')
Inputs may be any that keep to these rules, and one draw needn't show every extreme that they name: `seq_lengths`: row p lists the lengths of up to 4 sequences packed in order into given pack p; they sum to 1024; a zero is an unused entry; the first entry is at least 769, and some pack is one whole sequence. A permutation of the 16 packs; dealt slot j holds given pack deal_order[j]; the slots 2 * g to 2 * g + 1 belong to index g of dp.
All inputs are finite; a program needn't handle non-finite values.
Results may differ from a plain program's by a relative error of at most 0.018.
Values may be sent and summed in bfloat16 or wider, within the bound.
A program may use at most 256 MiB of HBM per device.

v0:
```python
import jax
import jax.numpy as jnp
from jax import lax
from jax.sharding import PartitionSpec as P

FF = 2048
QUERY_HEADS = 8
KEY_VALUE_HEADS = 2
HEAD_WIDTH = 64
MH = 24
HP = 64
NS = 128
STRETCH = 256
QBLOCK = 512


EPS = 1e-05
THETA = 100000000000.0
HIGH_PRECISION = lax.Precision.HIGHEST


def round_plain(v):
    return lax.optimization_barrier(v.astype(jnp.bfloat16)).astype(jnp.float32)


def value_keep(v):
    return (round_plain(v), None)


def value_pass(kept, grad):
    return (grad,)


def same_value(v):
    return v


def grad_keep(v):
    return (v, None)


def grad_narrow(kept, grad):
    return (round_plain(grad),)


def narrow_value(v):
    rounder = jax.custom_vjp(round_plain)
    rounder.defvjp(value_keep, value_pass)
    return rounder(v)


def narrow_grad(v):
    passer = jax.custom_vjp(same_value)
    passer.defvjp(grad_keep, grad_narrow)
    return passer(v)


def rms_scale(value_rows, gain):
    return (
        value_rows
        * lax.rsqrt(jnp.mean(value_rows * value_rows, axis=-1, keepdims=True) + EPS)
        * gain
    )


def gate_mix(ssm_vals, z_vals):
    return ssm_vals * jax.nn.silu(z_vals)


def swiglu(gate_vals):
    return jax.nn.silu(gate_vals[:, :FF]) * gate_vals[:, FF:]


def segments(lengths, seq_len):
    seq_ends = jnp.cumsum(lengths, axis=-1)[..., :-1]
    places = jnp.arange(seq_len, dtype=jnp.int32)
    return jnp.sum((places[None, :, None] >= seq_ends[:, None, :]).astype(jnp.int32), axis=-1)


def rotate(value_rows, places):
    half_dim = value_rows.shape[-1] // 2
    frequency = THETA ** (-jnp.arange(half_dim, dtype=jnp.float32) * 2.0 / value_rows.shape[-1])
    angles = places.astype(jnp.float32)[:, None] * frequency[None, :]
    cosine = jnp.cos(angles)[None, :, None, :]
    sine_vals = jnp.sin(angles)[None, :, None, :]
    lower_half = value_rows[..., :half_dim]
    upper_half = value_rows[..., half_dim:]
    return jnp.concatenate(
        [
            lower_half * cosine - upper_half * sine_vals,
            upper_half * cosine + lower_half * sine_vals,
        ],
        axis=-1,
    )


def attention(queries, key_rows, value_rows, seg_ids):
    num_packs, seq_len, num_heads, head_width = queries.shape
    places = jnp.arange(seq_len, dtype=jnp.int32)
    queries = rotate(queries, places)
    key_rows = rotate(key_rows[:, :, None, :], places)[:, :, 0, :]
    blocks = seq_len // QBLOCK
    q_blocks = jnp.moveaxis(queries.reshape(num_packs, blocks, QBLOCK, num_heads, head_width), 1, 0)
    seg_blocks = jnp.moveaxis(seg_ids.reshape(num_packs, blocks, QBLOCK), 1, 0)
    place_blocks = places.reshape(blocks, QBLOCK)

    def one_block(inputs):
        query_block, seg_block, place_block = inputs
        score_matrix = jnp.einsum(
            "rgce,rme->rcgm", query_block, key_rows, precision=HIGH_PRECISION
        ) * head_width ** (-0.5)
        score_matrix = narrow_grad(score_matrix)
        causal = (place_block[:, None] >= places[None, :])[None, None]
        same_seq = (seg_block[:, :, None] == seg_ids[:, None, :])[:, None]
        masked = jnp.where(causal & same_seq, score_matrix, -jnp.inf)
        row_top = jnp.max(masked, axis=-1, keepdims=True)
        weights = jnp.exp(masked - row_top)
        group_shares = narrow_value(weights / jnp.sum(weights, axis=-1, keepdims=True))
        return jnp.einsum("jnft,jtm->jfnm", group_shares, value_rows, precision=HIGH_PRECISION)

    results = lax.map(jax.checkpoint(one_block), (q_blocks, seg_blocks, place_blocks))
    return jnp.moveaxis(results, 0, 1).reshape(num_packs, seq_len, num_heads * head_width)


def scan_heads(inputs_x, inputs_b, inputs_c, dt_raw, bias_dt, log_a, skip_d, seg_ids):
    num_packs, seq_len, num_heads, head_width = inputs_x.shape
    dt_vals = jax.nn.softplus(dt_raw + bias_dt)
    log_decay = -dt_vals * jnp.exp(log_a)
    scaled_x = inputs_x * dt_vals[..., None]
    blocks = seq_len // STRETCH

    def to_blocks(value_rows):
        return jnp.moveaxis(
            value_rows.reshape((num_packs, blocks, STRETCH) + value_rows.shape[2:]), 1, 0
        )

    tri_mask = jnp.arange(STRETCH)[:, None] >= jnp.arange(STRETCH)[None, :]

    def stretch_step(carry, inputs):
        carry_state, prev_seg = carry
        x_scaled, b_part, c_part, decay_log, seg_part = inputs
        cum_log = jnp.cumsum(decay_log, axis=1)
        same_seg = (seg_part[:, :, None] == seg_part[:, None, :]) & tri_mask[None]
        spread = jnp.exp(
            jnp.where(
                same_seg[..., None], cum_log[:, :, None, :] - cum_log[:, None, :, :], -jnp.inf
            )
        )
        inner_prod = jnp.einsum("btn,bsn->bts", c_part, b_part, precision=HIGH_PRECISION)
        mixing = inner_prod[..., None] * spread
        local_y = jnp.einsum("btsm,bsmp->btmp", mixing, x_scaled, precision=HIGH_PRECISION)
        carried = (seg_part == prev_seg[:, None]).astype(jnp.float32)
        from_state = jnp.einsum("btn,bmpn->btmp", c_part, carry_state, precision=HIGH_PRECISION)
        local_y = local_y + from_state * (jnp.exp(cum_log) * carried[..., None])[..., None]
        last_seg = seg_part[:, -1]
        end_same = (seg_part == last_seg[:, None])[..., None]
        to_end = jnp.exp(jnp.where(end_same, cum_log[:, -1:, :] - cum_log, -jnp.inf))
        keep_state = (
            jnp.exp(cum_log[:, -1, :]) * (last_seg == prev_seg).astype(jnp.float32)[:, None]
        )
        weighted_x = to_end[..., None] * x_scaled
        carry_state = carry_state * keep_state[..., None, None] + jnp.einsum(
            "bsmp,bsn->bmpn", weighted_x, b_part, precision=HIGH_PRECISION
        )
        return ((carry_state, last_seg), local_y)

    start_carry = (
        jnp.zeros((num_packs, num_heads, head_width, inputs_b.shape[-1]), inputs_x.dtype),
        jnp.full((num_packs,), -1, jnp.int32),
    )
    ignored, outputs = lax.scan(
        jax.checkpoint(stretch_step),
        start_carry,
        (
            to_blocks(scaled_x),
            to_blocks(inputs_b),
            to_blocks(inputs_c),
            to_blocks(log_decay),
            to_blocks(seg_ids),
        ),
    )
    result = jnp.moveaxis(outputs, 0, 1).reshape(inputs_x.shape) + skip_d[:, None] * inputs_x
    return result.reshape(num_packs, seq_len, num_heads * head_width)


def rows_dot(left, right):
    return jnp.einsum("ti,io->to", left, right, preferred_element_type=jnp.float32)


def back_dot(left, right):
    return jnp.einsum("to,io->ti", left, right, preferred_element_type=jnp.float32)


def outer_dot(left, right):
    return jnp.einsum("ti,to->io", left, right, preferred_element_type=jnp.float32)


def body(
    tokens,
    cotangent,
    seq_lengths,
    deal_order,
    in_gain,
    in_proj,
    dt_proj,
    dt_bias,
    a_log,
    d_skip,
    ssm_out,
    attn_out,
    ffn_gain,
    gate_up,
    down_proj,
):
    head_groups = lax.axis_size("seq")
    dp_count = lax.axis_size("dp")
    group_index = lax.axis_index("seq")
    dp_index = lax.axis_index("dp")
    num_packs, span_len, model_width = cotangent.shape
    count_of_rows = num_packs * span_len
    seq_len = span_len * head_groups
    inner_dim = MH * HP
    query_group = QUERY_HEADS // head_groups
    m_group = MH // head_groups
    q_width = query_group * HEAD_WIDTH
    x_width = m_group * HP
    group_key_value = (
        jnp.arange(head_groups, dtype=jnp.int32) * query_group // (QUERY_HEADS // KEY_VALUE_HEADS)
    )
    dealt = jnp.take(tokens, deal_order, axis=0)
    arrived = lax.all_to_all(dealt, "dp", split_axis=0, concat_axis=2, tiled=True)
    gathered = (
        lax.all_gather(in_gain, "dp", axis=0, tiled=True),
        lax.all_gather(in_proj, "dp", axis=0, tiled=True),
        lax.all_gather(dt_proj, "dp", axis=0, tiled=True),
        lax.all_gather(ssm_out, "dp", axis=0, tiled=True),
        lax.all_gather(attn_out, "dp", axis=0, tiled=True),
        lax.all_gather(ffn_gain, "dp", axis=0, tiled=True),
        lax.all_gather(gate_up, "dp", axis=0, tiled=True),
        lax.all_gather(down_proj, "dp", axis=0, tiled=True),
    )
    gain_in, proj_in, proj_dt, proj_ssm, proj_attn, gain_ffn, proj_gu, proj_down = gathered
    residual = arrived.reshape(count_of_rows, model_width).astype(jnp.float32)
    normed_full, norm_back = jax.vjp(rms_scale, residual, gain_in.astype(jnp.float32))
    normed = normed_full.astype(jnp.bfloat16)
    projected = rows_dot(normed, proj_in).astype(jnp.bfloat16)
    dt_raw = rows_dot(normed, proj_dt).astype(jnp.bfloat16)
    z_part = projected[:, :inner_dim]
    x_part = projected[:, inner_dim : 2 * inner_dim]
    bc_part = projected[:, 2 * inner_dim : 2 * inner_dim + 2 * NS]
    q_start = 2 * inner_dim + 2 * NS
    key_offset = q_start + QUERY_HEADS * HEAD_WIDTH
    value_offset = key_offset + KEY_VALUE_HEADS * HEAD_WIDTH
    q_part = projected[:, q_start:key_offset]
    key_portion = projected[:, key_offset:value_offset]
    value_portion = projected[:, value_offset:]
    attn_tok = jnp.concatenate(
        [
            q_part.reshape(count_of_rows, head_groups, q_width),
            jnp.take(
                key_portion.reshape(count_of_rows, KEY_VALUE_HEADS, HEAD_WIDTH),
                group_key_value,
                axis=1,
            ),
            jnp.take(
                value_portion.reshape(count_of_rows, KEY_VALUE_HEADS, HEAD_WIDTH),
                group_key_value,
                axis=1,
            ),
        ],
        axis=-1,
    ).reshape(num_packs, span_len, -1)
    ssm_tok = jnp.concatenate(
        [
            x_part.reshape(count_of_rows, head_groups, x_width),
            jnp.broadcast_to(bc_part[:, None, :], (count_of_rows, head_groups, 2 * NS)),
        ],
        axis=-1,
    ).reshape(num_packs, span_len, -1)
    dt_tok = dt_raw.reshape(num_packs, span_len, MH)
    attn_head, ssm_head, dt_head = (
        lax.all_to_all(attn_tok, "seq", split_axis=2, concat_axis=1, tiled=True),
        lax.all_to_all(ssm_tok, "seq", split_axis=2, concat_axis=1, tiled=True),
        lax.all_to_all(dt_tok, "seq", split_axis=2, concat_axis=1, tiled=True),
    )
    pack_ids = lax.dynamic_slice_in_dim(deal_order, dp_index * num_packs, num_packs)
    seg_ids = segments(jnp.take(seq_lengths, pack_ids, axis=0), seq_len)
    head_start = group_index * m_group
    head_par = tuple(
        (
            lax.dynamic_slice_in_dim(vector, head_start, m_group)
            for vector in (dt_bias, a_log, d_skip)
        )
    )

    def mixer(attn_in, ssm_in, dt_in, params_head):
        queries = attn_in[..., :q_width].reshape(num_packs, seq_len, query_group, HEAD_WIDTH)
        key_rows = attn_in[..., q_width : q_width + HEAD_WIDTH]
        value_rows = attn_in[..., q_width + HEAD_WIDTH :]
        attn_vals = attention(queries, key_rows, value_rows, seg_ids)
        inputs_x = ssm_in[..., :x_width].reshape(num_packs, seq_len, m_group, HP)
        ssm_vals = scan_heads(
            inputs_x,
            ssm_in[..., x_width : x_width + NS],
            ssm_in[..., x_width + NS :],
            dt_in,
            params_head[0],
            params_head[1],
            params_head[2],
            seg_ids,
        )
        return (attn_vals, ssm_vals)

    mixed, mixer_back = jax.vjp(
        mixer,
        attn_head.astype(jnp.float32),
        ssm_head.astype(jnp.float32),
        dt_head.astype(jnp.float32),
        head_par,
    )
    attn_back_tok, ssm_back_tok = (
        lax.all_to_all(
            mixed[0].astype(jnp.bfloat16), "seq", split_axis=1, concat_axis=2, tiled=True
        ),
        lax.all_to_all(
            mixed[1].astype(jnp.bfloat16), "seq", split_axis=1, concat_axis=2, tiled=True
        ),
    )
    attn_rows = attn_back_tok.reshape(count_of_rows, QUERY_HEADS * HEAD_WIDTH)
    ssm_rows = ssm_back_tok.reshape(count_of_rows, inner_dim)
    gated_full, gated_back = jax.vjp(
        gate_mix, ssm_rows.astype(jnp.float32), z_part.astype(jnp.float32)
    )
    gated_vals = gated_full.astype(jnp.bfloat16)
    middle = residual + rows_dot(gated_vals, proj_ssm) + rows_dot(attn_rows, proj_attn)
    normed_two_full, norm_two_back = jax.vjp(rms_scale, middle, gain_ffn.astype(jnp.float32))
    normed_two = normed_two_full.astype(jnp.bfloat16)
    gate_vals = rows_dot(normed_two, proj_gu).astype(jnp.bfloat16)
    acted_full, act_back = jax.vjp(swiglu, gate_vals.astype(jnp.float32))
    acted_vals = acted_full.astype(jnp.bfloat16)
    output = (
        (middle + rows_dot(acted_vals, proj_down))
        .astype(jnp.bfloat16)
        .reshape(num_packs, span_len, model_width)
    )
    grad_out = cotangent.reshape(count_of_rows, model_width)
    grad_down = outer_dot(acted_vals, grad_out)
    grad_acted = back_dot(grad_out, proj_down).astype(jnp.bfloat16)
    grad_gate_full = act_back(grad_acted.astype(jnp.float32))[0]
    grad_gate_vals = grad_gate_full.astype(jnp.bfloat16)
    grad_gu = outer_dot(normed_two, grad_gate_vals)
    grad_normed_two = back_dot(grad_gate_vals, proj_gu).astype(jnp.bfloat16)
    grad_mid_norm, grad_gain_ffn = norm_two_back(grad_normed_two.astype(jnp.float32))
    grad_middle = grad_out.astype(jnp.float32) + grad_mid_norm
    grad_branch = grad_middle.astype(jnp.bfloat16)
    grad_ssm_proj = outer_dot(gated_vals, grad_branch)
    grad_attn_proj = outer_dot(attn_rows, grad_branch)
    grad_gated = back_dot(grad_branch, proj_ssm).astype(jnp.bfloat16)
    grad_attn_rows = back_dot(grad_branch, proj_attn).astype(jnp.bfloat16)
    grad_ssm_full, grad_z_full = gated_back(grad_gated.astype(jnp.float32))
    grad_ssm_rows = grad_ssm_full.astype(jnp.bfloat16)
    grad_z = grad_z_full.astype(jnp.bfloat16)
    grad_attn_tok = grad_attn_rows.reshape(num_packs, span_len, QUERY_HEADS * HEAD_WIDTH)
    grad_ssm_tok = grad_ssm_rows.reshape(num_packs, span_len, inner_dim)
    grad_attn_head, grad_ssm_head = (
        lax.all_to_all(grad_attn_tok, "seq", split_axis=2, concat_axis=1, tiled=True),
        lax.all_to_all(grad_ssm_tok, "seq", split_axis=2, concat_axis=1, tiled=True),
    )
    head_grads = mixer_back((grad_attn_head.astype(jnp.float32), grad_ssm_head.astype(jnp.float32)))
    grad_attn_in, grad_ssm_in, grad_dt_in, grad_par = head_grads
    attn_grad_tok, ssm_grad_tok, dt_grad_tok = (
        lax.all_to_all(
            grad_attn_in.astype(jnp.bfloat16), "seq", split_axis=1, concat_axis=2, tiled=True
        ),
        lax.all_to_all(
            grad_ssm_in.astype(jnp.bfloat16), "seq", split_axis=1, concat_axis=2, tiled=True
        ),
        lax.all_to_all(
            grad_dt_in.astype(jnp.bfloat16), "seq", split_axis=1, concat_axis=2, tiled=True
        ),
    )
    attn_grad_rows = attn_grad_tok.reshape(count_of_rows, head_groups, q_width + 2 * HEAD_WIDTH)
    grad_q = attn_grad_rows[..., :q_width].reshape(count_of_rows, QUERY_HEADS * HEAD_WIDTH)
    key_value_pick = (
        group_key_value[:, None] == jnp.arange(KEY_VALUE_HEADS, dtype=jnp.int32)[None, :]
    ).astype(jnp.float32)
    key_value_gradient = jnp.einsum(
        "tgd,gh->thd",
        attn_grad_rows[..., q_width:].astype(jnp.float32),
        key_value_pick,
        precision=HIGH_PRECISION,
    )
    key_gradient = (
        key_value_gradient[..., :HEAD_WIDTH]
        .reshape(count_of_rows, KEY_VALUE_HEADS * HEAD_WIDTH)
        .astype(jnp.bfloat16)
    )
    value_gradient = (
        key_value_gradient[..., HEAD_WIDTH:]
        .reshape(count_of_rows, KEY_VALUE_HEADS * HEAD_WIDTH)
        .astype(jnp.bfloat16)
    )
    ssm_grad_rows = ssm_grad_tok.reshape(count_of_rows, head_groups, x_width + 2 * NS)
    grad_x = ssm_grad_rows[..., :x_width].reshape(count_of_rows, inner_dim)
    grad_bc = jnp.sum(ssm_grad_rows[..., x_width:].astype(jnp.float32), axis=1).astype(jnp.bfloat16)
    grad_proj = jnp.concatenate(
        [grad_z, grad_x, grad_bc, grad_q, key_gradient, value_gradient], axis=-1
    )
    grad_dt_rows = dt_grad_tok.reshape(count_of_rows, MH)
    grad_in_mat = outer_dot(normed, grad_proj)
    grad_dt_mat = outer_dot(normed, grad_dt_rows)
    grad_normed = (back_dot(grad_proj, proj_in) + back_dot(grad_dt_rows, proj_dt)).astype(
        jnp.bfloat16
    )
    grad_res_norm, grad_gain_in = norm_back(grad_normed.astype(jnp.float32))
    grad_resid = (
        (grad_middle + grad_res_norm).astype(jnp.bfloat16).reshape(num_packs, span_len, model_width)
    )
    returned = lax.all_to_all(grad_resid, "dp", split_axis=2, concat_axis=0, tiled=True)
    grad_tokens = jnp.take(returned, jnp.argsort(deal_order), axis=0)
    matrices = (grad_in_mat, grad_dt_mat, grad_ssm_proj, grad_attn_proj, grad_gu, grad_down)
    shards = (
        lax.psum_scatter(matrices[0], "dp", scatter_dimension=0, tiled=True),
        lax.psum_scatter(matrices[1], "dp", scatter_dimension=0, tiled=True),
        lax.psum_scatter(matrices[2], "dp", scatter_dimension=0, tiled=True),
        lax.psum_scatter(matrices[3], "dp", scatter_dimension=0, tiled=True),
        lax.psum_scatter(matrices[4], "dp", scatter_dimension=0, tiled=True),
        lax.psum_scatter(matrices[5], "dp", scatter_dimension=0, tiled=True),
    )
    shards = (
        lax.psum(shards[0].astype(jnp.bfloat16), "seq").astype(jnp.float32),
        lax.psum(shards[1].astype(jnp.bfloat16), "seq").astype(jnp.float32),
        lax.psum(shards[2].astype(jnp.bfloat16), "seq").astype(jnp.float32),
        lax.psum(shards[3].astype(jnp.bfloat16), "seq").astype(jnp.float32),
        lax.psum(shards[4].astype(jnp.bfloat16), "seq").astype(jnp.float32),
        lax.psum(shards[5].astype(jnp.bfloat16), "seq").astype(jnp.float32),
    )
    head_stack = lax.dynamic_update_slice(
        jnp.zeros((3, MH), jnp.float32), jnp.stack(grad_par), (0, head_start)
    )
    head_sums, gain_in_sum, gain_ffn_sum = lax.psum(
        (head_stack, grad_gain_in, grad_gain_ffn), ("dp", "seq")
    )
    gain_rows = model_width // dp_count
    grad_in_gain = lax.dynamic_slice_in_dim(gain_in_sum, dp_index * gain_rows, gain_rows)
    grad_ffn_gain = lax.dynamic_slice_in_dim(gain_ffn_sum, dp_index * gain_rows, gain_rows)
    return (
        output,
        grad_tokens,
        grad_in_gain,
        shards[0],
        shards[1],
        head_sums[0],
        head_sums[1],
        head_sums[2],
        shards[2],
        shards[3],
        grad_ffn_gain,
        shards[4],
        shards[5],
    )


def solution(mesh):
    return jax.shard_map(
        body,
        mesh=mesh,
        in_specs=(
            P(None, "seq", "dp"),
            P("dp", "seq", None),
            P(),
            P(),
            P("dp"),
            P("dp", None),
            P("dp", None),
            P(),
            P(),
            P(),
            P("dp", None),
            P("dp", None),
            P("dp"),
            P("dp", None),
            P("dp", None),
        ),
        out_specs=(
            P("dp", "seq", None),
            P(None, "seq", "dp"),
            P("dp"),
            P("dp", None),
            P("dp", None),
            P(),
            P(),
            P(),
            P("dp", None),
            P("dp", None),
            P("dp"),
            P("dp", None),
            P("dp", None),
        ),
        check_vma=False,
    )
```

profile of v0, /device:TPU:9, one launch (start us, length us, event | category | flops | bytes accessed | tf_op | source)
XLA Modules:
  0.0 1582.8 jit_solution(15116372756752317943)
XLA Ops:
  13.4 5.7 all-to-all-start
  20.6 54.8 %all-gather = bf16[8,1,128]{2,1,0:T(2,128)(2,1)S(1)} all-gather(bf16[1,1,128]{2,1,0:T(2,128)(2,1)S(1)} %bitcast.869), channel_id=1, replica_groups=mesh['dp'=8,'seq'=4] {'dp'}, dimensions={0}, use_global_device_ids=true | all-gather | bytes 2304 | tf_op jit(solution)/shard_map/all_gather | solution.py:233
  76.7 20.9 %all_gather.25 = bf16[1024,24]{0,1:T(8,128)(2,1)S(1)} all-gather(bf16[128,24]{0,1:T(8,128)(2,1)S(1)} %copy-done.78), channel_id=1, replica_groups=mesh['dp'=8,'seq'=4] {'dp'}, dimensions={0}, use_global_device_ids=true | all-gather | bytes 55296 | tf_op jit(solution)/shard_map/all_gather | solution.py:235
  106.1 12.9 all-to-all-start.1
  119.1 36.7 %all-gather.8.cloned.1.call-done = bf16[1024,4096]{1,0:T(8,128)(2,1)} async-done(((bf16[128,4096]{1,0:T(8,128)(2,1)}), bf16[1024,4096]{1,0:T(8,128)(2,1)}) %all-gather.8.cloned.1.call-update) | async-done | bytes 8388624 | tf_op jit(solution)/shard_map/all_gather | solution.py:234
  155.7 8.1 convolution_convert_fusion.1
  172.0 5.5 all-to-all-start.4
  189.4 5.5 reshape.763
  194.9 7.4 copy.962
  225.5 53.6 %while.74 = (s32[]{:T(128)}, bf16[2,2,512,2,64]{2,4,3,1,0:T(8,128)(2,1)}, s32[2,512]{1,0:T(2,128)S(1)}, s32[2,2,512]{2,1,0:T(2,128)S(1)}, s32[2,1,1024]{2,0,1:T(...) while((s32[]{:T(128)}, ...), condition=%wide.region_10.13_spmd.clone, body=%wide.region_7.12_spmd.clone.sunk | while | flops 3240625152 | bytes 53520584 | solution.py:121
  225.7 7.9 fusion.329
  235.8 7.3 fusion.330
  252.0 7.9 fusion.329
  262.1 7.3 fusion.330
  291.8 5.9 copy.964
  306.7 5.1 reshape.764
  321.4 79.0 %while.75 = (s32[]{:T(128)}, f32[2,6,64,128]{3,2,1,0:T(8,128)S(1)}, s32[2]{0:T(128)S(1)}, f32[4,2,256,6,64]{2,4,3,1,0:T(8,128)}, f32[4,2,6,64,128]{4,3,2,1,0:T(8...) while((s32[]{:T(128)}, f32[2,6,64,128]{3,2,1,0:T(8,128)S(1)}, ...), condition=%wide.region_6.8_spmd.clone, body=%wide.region_3.7_spmd.clone.sunk | while | flops 1413458432 | bytes 8747843 | solution.py:171
  400.4 5.6 copy.971
  406.0 5.2 reshape.767
  424.7 13.7 all-gather.1
  452.0 5.6 fusion.220
  461.8 11.8 fusion.141
  473.7 13.0 convert_multiply_fusion.4
  486.7 11.3 fusion.160
  502.2 6.1 fusion.223
  508.3 7.7 fusion.224
  525.4 8.2 fusion.166
  533.6 8.5 fusion.171
  560.3 122.0 %while.77 = (s32[]{:T(128)}, f32[2,1024,64]{1,2,0:T(8,128)}, f32[2,1024,64]{1,2,0:T(8,128)}, f32[2,2,512,2,64]{2,4,3,1,0:T(8,128)}, f32[2,2,512,2,64]{2,4,3,1,0:...) while((s32[]{:T(128)}, f32[2,1024,64]{1,2,0:T(8,128)}, ...), condition=%wide.region_33.36_spmd.clone, body=%wide.region_27.35_spmd.clone.sunk | while | flops 8137998336 | bytes 155404656 | solution.py:121
  563.8 8.9 fusion.376
  575.5 9.2 multiply_reduce_fusion.12
  584.7 5.5 convert_reduce_fusion.2
  590.3 6.5 divide_convert_fusion.5
  596.8 9.0 fusion.378
  608.9 8.6 fusion.380
  622.3 8.9 fusion.376
  633.8 9.2 multiply_reduce_fusion.12
  643.0 5.5 convert_reduce_fusion.2
  648.5 6.7 divide_convert_fusion.5
  655.3 9.1 fusion.378
  668.7 8.6 fusion.380
  710.1 246.2 %while.76 = (s32[]{:T(128)}, f32[2,6,64,128]{3,2,1,0:T(8,128)}, f32[4,2,256,6,64]{2,4,3,1,0:T(8,128)}, f32[4,2,256,128]{3,2,0,1:T(8,128)}, f32[4,2,256,128]{3,2,...) while((s32[]{:T(128)}, f32[2,6,64,128]{3,2,1,0:T(8,128)}, ...), condition=%wide.region_25.28_spmd.clone, body=%wide.region_13.27_spmd.clone.sunk | while | flops 3334748672 | bytes 25757532 | solution.py:171
  723.7 5.9 fusion.363
  755.1 15.1 reduce-window.78
  785.4 5.9 fusion.363
  816.8 15.1 reduce-window.78
  847.0 5.9 fusion.363
  878.4 15.1 reduce-window.78
  908.7 5.9 fusion.363
  940.1 15.1 reduce-window.78
  956.3 5.8 copy.1002
  962.1 5.2 reshape.784
  984.6 5.7 fusion.153
  1003.4 26.6 %all-to-all-done.7 = bf16[2,1024,640]{2,0,1:T(2,128)(2,1)} async-done(((bf16[2,1024,640]{2,0,1:T(2,128)(2,1)}), bf16[2,1024,640]{2,0,1:T(2,128)(2,1)}, u32[]{:S(2)}, u32[]{:S(2)}) %all-to-all-start.7) | async-done | bytes 2621472 | tf_op jit(solution)/shard_map/all_to_all | solution.py:375
  1037.1 8.4 fusion.222
  1056.2 8.4 fusion.221
  1072.8 5.1 all-to-all-start.11
  1086.0 61.1 %reduce-scatter.15.cloned.1.call-done = f32[128,4096]{1,0:T(8,128)} async-done(((f32[1024,4096]{1,0:T(8,128)}), f32[128,4096]{1,0:T(8,128)}) %reduce-scatter.15.cloned.1.call-update) | async-done | bytes 2097168 | tf_op jit(solution)/shard_map/reduce_scatter | solution.py:427
  1149.8 283.4 %reduce-scatter.7.cloned.1.call-done = f32[128,4096]{1,0:T(8,128)} async-done(((f32[1024,4096]{1,0:T(8,128)}), f32[128,4096]{1,0:T(8,128)}) %reduce-scatter.7.cloned.1.call-update) | async-done | bytes 2097168 | tf_op jit(solution)/shard_map/reduce_scatter | solution.py:423
  1435.9 6.1 add_convert_fusion.5
  1443.0 50.6 %reduce-scatter.9.cloned.1.call-done = f32[128,24]{0,1:T(8,128)} async-done(((f32[1024,24]{0,1:T(8,128)}), f32[128,24]{0,1:T(8,128)}) %reduce-scatter.9.cloned.1.call-update) | async-done | bytes 12304 | tf_op jit(solution)/shard_map/reduce_scatter | solution.py:424
  1494.3 7.8 psum.65
  1502.7 39.3 %all-reduce.14 = (f32[1024]{0:T(1024)S(1)}, f32[3,24]{1,0:T(4,128)S(1)}, f32[1024]{0:T(1024)S(1)}) all-reduce(f32[1024]{0:T(1024)S(1)} %get-tuple-element.1328, f32[3,24]{1,0:T(4,128)S(1)} %dynamic_update_slice.74, f32[1024]{0:T(1024)S(1)} %copy-done.81), channel_id=1, replica_groups=mesh['dp'=8,'seq'=4] {'dp','seq'}, use_global_device_ids=true, to_apply=%region_38.41 | all-reduce | flops 2120 | bytes 16960 | tf_op jit(solution)/shard_map/psum | solution.py:441
  1546.5 22.0 %all-reduce.18.cloned.1.call-done = (bf16[128,4096]{1,0:T(8,128)(2,1)}, bf16[192,1024]{1,0:T(8,128)(2,1)}, bf16[64,1024]{1,0:T(8,128)(2,1)}, bf16[128,4096]{1,0:T(8,128)(2,1)}, bf16[256,1024]{1,0:T(8,128)(2,1)}) async-done(((bf16[128,4096]{1,0:T(8,128)(2,1)}, bf16[192,1024]{1,0:T(8,128)(2,1)}, bf16[64,1024]{1,0:T(8,128)(2,1)}, bf16[128,4096]{1,0:T(8,128)(2,1)}, bf16[256,1024]{1,0:T(8,128)(2,1)}), ...) | async-done | bytes 3145744 | tf_op jit(solution)/shard_map/psum | solution.py:431
  (860 shorter events, 548.7 us)
Async XLA Ops:
  7.2 148.5 %all-gather.8.cloned.1.call-start = ((), (), s32[]{:S(2)}) async-start(), calls=%async_computation.18 | async-start | bytes 9437184 | tf_op jit(solution)/shard_map/all_gather | solution.py:234
  7.9 444.1 %all-gather.10.cloned.1.call-start = ((), (), s32[]{:S(2)}) async-start(), calls=%async_computation.19 | async-start | bytes 3538944 | tf_op jit(solution)/shard_map/all_gather | solution.py:236
  8.7 449.0 %all-gather.12.cloned.1.call-start = ((), (), s32[]{:S(2)}) async-start(), calls=%async_computation.20 | async-start | bytes 1179648 | tf_op jit(solution)/shard_map/all_gather | solution.py:237
  9.4 452.4 %all-gather.14.cloned.1.call-start = ((), (), s32[]{:S(2)}) async-start(), calls=%async_computation.21 | async-start | bytes 9437184 | tf_op jit(solution)/shard_map/all_gather | solution.py:239
  11.4 8.2 copy-start.82
  11.4 9.2 copy-start.83
  11.4 65.3 %copy-start.78 = (bf16[128,24]{0,1:T(8,128)(2,1)S(1)}, bf16[128,24]{0,1:T(8,128)(2,1)}, u32[]{:S(2)}) copy-start(bf16[128,24]{0,1:T(8,128)(2,1)} %param.33) | copy-start | bytes 18436
  13.4 86.4 %all-to-all-start = ((bf16[16,256,128]{2,1,0:T(8,128)(2,1)}), bf16[16,256,128]{2,1,0:T(8,128)(2,1)S(1)}, u32[]{:S(2)}, u32[]{:S(2)}) async-start(bf16[16,256,128]{2,1,0:T(8,128)(2,1)} %broadcast_select_fusion.2), calls=%async_computation | async-start | bytes 2097152 | tf_op jit(solution)/shard_map/all_to_all | solution.py:231
  19.1 454.6 %all-gather.16.cloned.1.call-start = ((), (), s32[]{:S(2)}) async-start(), calls=%async_computation.22 | async-start | bytes 4718592 | tf_op jit(solution)/shard_map/all_gather | solution.py:240
  75.5 27.9 %copy-start.60 = (f32[8,1,128]{2,1,0:T(1,128)}, f32[8,1,128]{2,1,0:T(1,128)S(1)}, u32[]{:S(2)}) copy-start(f32[8,1,128]{2,1,0:T(1,128)S(1)} %convert_element_type.483) | copy-start | bytes 12292
  76.7 26.6 %copy-start.90 = (s32[16]{0:T(128)}, s32[16]{0:T(128)S(1)}, u32[]{:S(2)}) copy-start(s32[16]{0:T(128)S(1)} %get-tuple-element.767) | copy-start | bytes 196
  97.6 7.5 copy-start.53
  99.7 77.8 %copy-start.42 = (f32[1024,32]{0,1:T(8,128)}, f32[1024,32]{0,1:T(8,128)S(1)}, u32[]{:S(2)}) copy-start(f32[1024,32]{0,1:T(8,128)S(1)} %get-tuple-element.1484) | copy-start | bytes 393220
  99.7 116.1 %copy-start.40 = (f32[1024,32]{0,1:T(8,128)}, f32[1024,32]{0,1:T(8,128)S(1)}, u32[]{:S(2)}) copy-start(f32[1024,32]{0,1:T(8,128)S(1)} %get-tuple-element.1483) | copy-start | bytes 393220
  105.1 58.7 %copy-start.17 = (bf16[512,1024]{1,0:T(8,128)(2,1)}, bf16[512,1024]{1,0:T(8,128)(2,1)S(1)}, u32[]{:S(2)}) copy-start(bf16[512,1024]{1,0:T(8,128)(2,1)S(1)} %multiply_convert_fusion.4) | copy-start | bytes 3145732
  106.1 65.9 %all-to-all-start.1 = ((bf16[2,256,24]{1,0,2:T(2,128)(2,1)}), bf16[2,256,24]{1,0,2:T(2,128)(2,1)S(1)}, u32[]{:S(2)}, u32[]{:S(2)}) async-start(bf16[2,256,24]{1,0,2:T(2,128)(2,1)} %reshape.760), calls=%async_computation.1 | async-start | bytes 49152 | tf_op jit(solution)/shard_map/all_to_all | solution.py:284
  169.2 8.3 copy-start.86
  169.9 8.8 copy-start.88
  170.0 11.8 copy-start.89
  172.0 11.6 copy-start.49
  172.0 30.2 %all-to-all-start.4 = ((bf16[2,256,1024]{1,0,2:T(2,128)(2,1)}), bf16[2,256,1024]{1,0,2:T(2,128)(2,1)}, u32[]{:S(2)}, u32[]{:S(2)}) async-start(bf16[2,256,1024]{1,0,2:T(2,128)(2,1)} %copy.981), calls=%async_computation.4 | async-start | bytes 2097152 | tf_op jit(solution)/shard_map/all_to_all | solution.py:282
  177.6 6.0 copy-start.79
  177.6 6.0 slice-start.1
  177.8 44.8 %copy-start.21 = (f32[1024,32]{1,0:T(8,128)}, f32[1024,32]{1,0:T(8,128)S(1)}, u32[]{:S(2)}) copy-start(f32[1024,32]{1,0:T(8,128)S(1)} %copy.986) | copy-start | bytes 393220
  182.0 233.0 %copy-start.67 = (f32[384]{0:T(512)}, f32[384]{0:T(512)S(1)}, u32[]{:S(2)}) copy-start(f32[384]{0:T(512)S(1)} %mul.954) | copy-start | bytes 4612
  202.3 80.5 %all-to-all-start.2 = ((bf16[2,256,2560]{1,0,2:T(2,128)(2,1)}), bf16[2,256,2560]{1,0,2:T(2,128)(2,1)}, u32[]{:S(2)}, u32[]{:S(2)}) async-start(bf16[2,256,2560]{1,0,2:T(2,128)(2,1)} %copy.962), calls=%async_computation.2 | async-start | bytes 5242880 | tf_op jit(solution)/shard_map/all_to_all | solution.py:283
  216.1 6.5 copy-start.16
  216.1 6.5 copy-start.23
  282.7 138.2 %all-to-all-start.5 = ((bf16[2,1024,128]{2,0,1:T(2,128)(2,1)}), bf16[2,1024,128]{2,0,1:T(2,128)(2,1)}, u32[]{:S(2)}, u32[]{:S(2)}) async-start(bf16[2,1024,128]{2,0,1:T(2,128)(2,1)} %reshape.896), calls=%async_computation.5 | async-start | bytes 1048576 | tf_op jit(solution)/shard_map/all_to_all | solution.py:322
  418.2 6.5 copy-start.84
  420.9 23.0 %all-to-all-start.3 = ((bf16[2,1024,384]{2,0,1:T(2,128)(2,1)}), bf16[2,1024,384]{2,0,1:T(2,128)(2,1)S(1)}, u32[]{:S(2)}, u32[]{:S(2)}) async-start(bf16[2,1024,384]{2,0,1:T(2,128)(2,1)} %copy.973), calls=%async_computation.3 | async-start | bytes 3145728 | tf_op jit(solution)/shard_map/all_to_all | solution.py:325
  424.7 655.7 %reduce-scatter.13.cloned.1.call-start = ((), (), s32[]{:S(2)}) async-start(), calls=%async_computation.26 | async-start | bytes 2359296 | tf_op jit(solution)/shard_map/reduce_scatter | solution.py:426
  438.4 95.2 %copy-start.63 = (f32[8,1,128]{2,1,0:T(1,128)}, f32[8,1,128]{2,1,0:T(1,128)S(1)}, u32[]{:S(2)}) copy-start(f32[8,1,128]{2,1,0:T(1,128)S(1)} %convert_element_type.484) | copy-start | bytes 12292
  461.8 71.8 %copy-start.73 = (f32[512]{0:T(512)}, f32[512]{0:T(512)S(1)}, u32[]{:S(2)}) copy-start(f32[512]{0:T(512)S(1)} %fusion.205) | copy-start | bytes 6148
  473.7 13.0 copy-start.13
  486.7 11.4 copy-start.35
  502.1 579.9 %reduce-scatter.11.cloned.1.call-start = ((), (), s32[]{:S(2)}) async-start(), calls=%async_computation.25 | async-start | bytes 7077888 | tf_op jit(solution)/shard_map/reduce_scatter | solution.py:425
  508.3 575.6 %reduce-scatter.17.cloned.1.call-start = ((), (), s32[]{:S(2)}) async-start(), calls=%async_computation.28 | async-start | bytes 9437184 | tf_op jit(solution)/shard_map/reduce_scatter | solution.py:428
  520.9 27.0 %all-to-all-start.8 = ((bf16[2,256,512]{1,0,2:T(2,128)(2,1)}), bf16[2,256,512]{1,0,2:T(2,128)(2,1)S(1)}, u32[]{:S(2)}, u32[]{:S(2)}) async-start(bf16[2,256,512]{1,0,2:T(2,128)(2,1)} %copy.1011), calls=%async_computation.8 | async-start | bytes 1048576 | tf_op jit(solution)/shard_map/all_to_all | solution.py:366
  525.0 622.1 %reduce-scatter.15.cloned.1.call-start = ((), (), s32[]{:S(2)}) async-start(), calls=%async_computation.27 | async-start | bytes 18874368 | tf_op jit(solution)/shard_map/reduce_scatter | solution.py:427
  525.4 8.2 copy-start.92
  525.4 8.2 copy-start.93
  548.7 143.3 %all-to-all-start.6 = ((bf16[2,256,1536]{1,0,2:T(2,128)(2,1)}), bf16[2,256,1536]{1,0,2:T(2,128)(2,1)}, u32[]{:S(2)}, u32[]{:S(2)}) async-start(bf16[2,256,1536]{1,0,2:T(2,128)(2,1)} %copy.993), calls=%async_computation.6 | async-start | bytes 3145728 | tf_op jit(solution)/shard_map/all_to_all | solution.py:367
  554.3 6.0 copy-start.7
  554.3 6.0 copy-start.11
  560.3 123.4 %copy-start.41 = (f32[1024,32]{0,1:T(8,128)S(1)}, f32[1024,32]{0,1:T(8,128)}, u32[]{:S(2)}) copy-start(f32[1024,32]{0,1:T(8,128)} %copy-done.40) | copy-start | bytes 393220
  560.3 123.4 %copy-start.44 = (f32[1024,32]{0,1:T(8,128)S(1)}, f32[1024,32]{0,1:T(8,128)}, u32[]{:S(2)}) copy-start(f32[1024,32]{0,1:T(8,128)} %copy-done.42) | copy-start | bytes 393220
  596.8 9.0 copy-start.3
  655.3 9.1 copy-start.3
  692.0 302.8 %all-to-all-start.9 = ((bf16[2,1024,256]{2,0,1:T(2,128)(2,1)}), bf16[2,1024,256]{2,0,1:T(2,128)(2,1)}, u32[]{:S(2)}, u32[]{:S(2)}) async-start(bf16[2,1024,256]{2,0,1:T(2,128)(2,1)} %copy.1022), calls=%async_computation.9 | async-start | bytes 2097152 | tf_op jit(solution)/shard_map/all_to_all | solution.py:372
  994.9 35.2 %all-to-all-start.7 = ((bf16[2,1024,640]{2,0,1:T(2,128)(2,1)}), bf16[2,1024,640]{2,0,1:T(2,128)(2,1)}, u32[]{:S(2)}, u32[]{:S(2)}) async-start(bf16[2,1024,640]{2,0,1:T(2,128)(2,1)} %copy.1007), calls=%async_computation.7 | async-start | bytes 5242880 | tf_op jit(solution)/shard_map/all_to_all | solution.py:375
  999.4 433.7 %reduce-scatter.7.cloned.1.call-start = ((), (), s32[]{:S(2)}) async-start(), calls=%async_computation.23 | async-start | bytes 18874368 | tf_op jit(solution)/shard_map/reduce_scatter | solution.py:423
  1047.4 7.2 all-to-all-start.10
  1056.1 8.5 copy-start.10
  1056.1 8.5 copy-start.54
  1056.2 8.5 copy-start.61
  1056.2 8.5 copy-start.66
  1069.1 11.2 copy-start.91
  1072.8 470.9 %all-to-all-start.11 = ((bf16[2,256,1024]{1,0,2:T(2,128)(2,1)}), bf16[2,256,1024]{1,0,2:T(2,128)(2,1)S(1)}, u32[]{:S(2)}, u32[]{:S(2)}) async-start(bf16[2,256,1024]{1,0,2:T(2,128)(2,1)} %copy.1034), calls=%async_computation.11 | async-start | bytes 2097152 | tf_op jit(solution)/shard_map/all_to_all | solution.py:419
  1077.8 415.8 %reduce-scatter.9.cloned.1.call-start = ((), (), s32[]{:S(2)}) async-start(), calls=%async_computation.24 | async-start | bytes 110592 | tf_op jit(solution)/shard_map/reduce_scatter | solution.py:424
  1080.0 488.5 %all-reduce.18.cloned.1.call-start = ((), (), s32[]{:S(2)}) async-start(), calls=%async_computation.29 | async-start | bytes 6291456 | tf_op jit(solution)/shard_map/psum | solution.py:431
  1435.9 6.4 copy-start.51
  1435.9 6.8 copy-start.87
  1435.9 66.9 %copy-start.81 = (f32[1024]{0:T(1024)S(1)}, f32[1024]{0:T(1024)}, u32[]{:S(2)}) copy-start(f32[1024]{0:T(1024)} %get-tuple-element.1326) | copy-start | bytes 12292
  (74 other events, 227.3 us)
Sparse Core Ops, SparseCore 0:
  10.2 145.5 all-gather.7
  157.9 59.4 all-gather.9
  219.5 38.3 all-gather.11
  259.9 123.0 all-gather.13
  385.0 72.2 all-gather.15
  502.2 64.9 reduce-scatter.12
  570.9 118.0 reduce-scatter.10
  692.6 147.5 reduce-scatter.16
  844.5 302.5 reduce-scatter.14
  1150.7 282.3 reduce-scatter.6
  1437.3 56.2 reduce-scatter.8
  1497.5 70.9 all-reduce.17
where the time goes:
time: 1600 us; the launch traced here: 1580 us
  waiting for transfers between devices  491 us (31%)
  matrix products  357 us (22%)
  other arithmetic  258 us (16%)
  local copies, waits for them, and re-layouts  254 us (16%)
  blocking collectives  136 us (8%)
  starting transfers between devices  64.2 us (4%)
  between operations  16 us (1%)
    reduce_scatter x1, waiting for transfers between devices, body(): lax.psum_scatter(matrices[0], 'dp', scatter_dimension=0, tiled=True)  283 us
    another operation x42, other arithmetic  97.4 us
    dot_general x8, matrix products, one_block(): jnp.einsum('rgce,rme->rcgm', query_block, key_rows, precision=HIGH_PRECIS...  69 us
    dot_general x12, matrix products, stretch_step(): jnp.einsum('btsm,bsmp->btmp', mixing, x_scaled, precision=HIGH_PRECISION)  61.8 us
    reduce_scatter x1, waiting for transfers between devices, body(): lax.psum_scatter(matrices[4], 'dp', scatter_dimension=0, tiled=True)  61.1 us
    all_gather x1, blocking collectives, body(): lax.all_gather(in_gain, 'dp', axis=0, tiled=True)  54.8 us
    reduce_scatter x1, waiting for transfers between devices, body(): lax.psum_scatter(matrices[1], 'dp', scatter_dimension=0, tiled=True)  50.6 us
    dot_general x6, matrix products, back_dot(): jnp.einsum('to,io->ti', left, right, preferred_element_type=jnp.float32)  44.2 us
  transfers between devices with their start and end apart: 24, of which 8 were waited for; matrix products, arithmetic and copies ran while one was open for 51% of the time, Pallas kernels for 0%

commit v1 on v0

v1 whole, which is shorter than its diff:
```python
import functools

import jax
import jax.numpy as jnp
from jax import lax
from jax.experimental import pallas as pl
from jax.experimental.pallas import tpu as pltpu
from jax.sharding import PartitionSpec as P

FF = 2048
QUERY_HEADS = 8
KEY_VALUE_HEADS = 2
HEAD_WIDTH = 64
MH = 24
HP = 64
NS = 128
EPS = 1e-05
THETA = 100000000000.0
BF = jnp.bfloat16
F32 = jnp.float32
CORES = 2
CHIP_HEADS = MH // CORES
XW = CHIP_HEADS * HP
QW = QUERY_HEADS // CORES * HEAD_WIDTH
Z0, X0, Q0, KV0, B0, C0, T0 = 0, XW, 2 * XW, 2 * XW + QW, 2 * XW + QW + 128, 2 * XW + QW + 256, 2 * XW + QW + 384
COLS = T0 + 128
CHUNK = 256
QB = 256
FAR = -1e30
MIB = 1 << 20
MESH = pl.DeviceIdType.MESH
VM = pltpu.VMEM


def dot(a, b, dims=((1,), (0,)), precision=None):
    return lax.dot_general(a, b, (dims, ((), ())), precision=precision, preferred_element_type=F32)


def lanes(rows, width=128):
    return lax.broadcasted_iota(jnp.int32, (rows, width), 1)


def swap_halves(v):
    low = lanes(v.shape[0], v.shape[1]) % 64 < 32
    return jnp.where(low, pltpu.roll(v, v.shape[1] - 32, 1), pltpu.roll(v, 32, 1))


def turn(v, cosine, sine):
    return v * cosine + swap_halves(v) * sine


def turn_back(v, cosine, sine):
    return v * cosine - swap_halves(v) * sine


def widen(v, spread):
    v = jnp.where(lanes(v.shape[0]) < 64, v, 0.0)
    top = v.astype(BF)
    rest = (v - top.astype(F32)).astype(BF).astype(F32)
    both = top.astype(F32) + pltpu.roll(rest, 64, 1)
    return dot(both.astype(BF), spread)


def attn_masks(segc_ref, segr_ref, i, upto):
    rows = pl.ds(i * QB, QB)
    same = segc_ref[rows, 0:1] == segr_ref[0:1, 0:upto]
    t = lax.broadcasted_iota(jnp.int32, (QB, upto), 0) + i * QB
    u = lax.broadcasted_iota(jnp.int32, (QB, upto), 1)
    return jnp.where(same & (u <= t), 0.0, FAR)


def key_value_pairs(kv, cosine, sine):
    low = lanes(kv.shape[0]) < 64
    other = pltpu.roll(kv, 64, 1)
    kk = turn(jnp.where(low, kv, other), cosine, sine)
    vv = jnp.where(low, other, kv)
    return kk.astype(BF), vv.astype(BF)


def attention_forward(proj_ref, cos_ref, sin_ref, segc_ref, segr_ref, attn_ref, lse_ref):
    seq_len = proj_ref.shape[0]
    kk, vv = key_value_pairs(proj_ref[:, KV0 : KV0 + 128].astype(F32), cos_ref[...], sin_ref[...])
    low = lanes(QB) < 64
    for i in range(seq_len // QB):
        rows = slice(i * QB, (i + 1) * QB)
        upto = (i + 1) * QB
        mask = attn_masks(segc_ref, segr_ref, i, upto)
        tops = jnp.zeros((QB, 128), F32)
        for pair in range(QW // 128):
            q = proj_ref[rows, Q0 + 128 * pair : Q0 + 128 * (pair + 1)].astype(F32)
            q = turn(q, cos_ref[rows, :], sin_ref[rows, :]) * HEAD_WIDTH**-0.5
            outs = []
            for half in range(2):
                qh = jnp.where(low if half == 0 else ~low, q, 0.0).astype(BF)
                s = dot(qh, kk[:upto], ((1,), (1,))) + mask
                top = jnp.max(s, axis=1, keepdims=True)
                e = jnp.exp(s - top)
                total = jnp.sum(e, axis=1, keepdims=True)
                outs.append(dot(e.astype(BF), vv[:upto]) / total)
                tops = jnp.where(lanes(QB) == 2 * pair + half, top + jnp.log(total), tops)
            attn_ref[rows, 128 * pair : 128 * (pair + 1)] = jnp.where(low, outs[0], outs[1]).astype(BF)
        lse_ref[rows, :] = tops


def attention_backward(proj_ref, cos_ref, sin_ref, segc_ref, segr_ref, attn_ref, lse_ref, gattn_ref, gproj_ref, gkv):
    seq_len = proj_ref.shape[0]
    kk, vv = key_value_pairs(proj_ref[:, KV0 : KV0 + 128].astype(F32), cos_ref[...], sin_ref[...])
    low = lanes(QB) < 64
    gkv[...] = jnp.zeros_like(gkv)
    pick = (lax.broadcasted_iota(jnp.int32, (QW, 128), 0) // 64 == lanes(QW)).astype(BF)
    for i in range(seq_len // QB):
        rows = slice(i * QB, (i + 1) * QB)
        upto = (i + 1) * QB
        same = segc_ref[0:upto, 0:1] == segr_ref[0:1, rows]
        t = lanes(upto, QB) + i * QB
        u = lax.broadcasted_iota(jnp.int32, (upto, QB), 0)
        mask = jnp.where(same & (u <= t), 0.0, FAR)
        weighed = gattn_ref[rows, :].astype(F32) * attn_ref[rows, :].astype(F32)
        deltas = dot(weighed.astype(BF), pick).T
        tops = lse_ref[rows, :].T
        for pair in range(QW // 128):
            cosine, sine = cos_ref[rows, :], sin_ref[rows, :]
            q = proj_ref[rows, Q0 + 128 * pair : Q0 + 128 * (pair + 1)].astype(F32)
            q = turn(q, cosine, sine) * HEAD_WIDTH**-0.5
            g = gattn_ref[rows, 128 * pair : 128 * (pair + 1)]
            grads = []
            for half in range(2):
                head = 2 * pair + half
                mine = low if half == 0 else ~low
                qh = jnp.where(mine, q, 0.0).astype(BF)
                gh = jnp.where(mine, g, jnp.zeros_like(g))
                s = dot(kk[:upto], qh, ((1,), (1,))) + mask
                p = jnp.exp(s - tops[head : head + 1, :])
                gp = dot(vv[:upto], gh, ((1,), (1,)))
                gs = (p * (gp - deltas[head : head + 1, :])).astype(BF)
                gkv[0:upto, 0:128] += dot(gs, qh)
                gkv[0:upto, 128:256] += dot(p.astype(BF), gh)
                grads.append(dot(gs, kk[:upto], ((0,), (0,))))
            gq = jnp.where(low, grads[0], grads[1]) * HEAD_WIDTH**-0.5
            gproj_ref[rows, Q0 + 128 * pair : Q0 + 128 * (pair + 1)] = turn_back(gq, cosine, sine).astype(BF)
    gk = gkv[:, 0:128]
    gv = gkv[:, 128:256]
    gk = turn_back(gk + pltpu.roll(gk, 64, 1), cos_ref[...], sin_ref[...])
    gv = gv + pltpu.roll(gv, 64, 1)
    gproj_ref[:, KV0 : KV0 + 128] = jnp.where(lanes(seq_len) < 64, gk, gv).astype(BF)


def scan_pieces(j, proj_ref, segc_ref, segr_ref, par_ref):
    rows = pl.ds(pl.multiple_of(j * CHUNK, CHUNK), CHUNK)
    seg = segc_ref[rows, :]
    prev = segc_ref[pl.ds(jnp.maximum(j * CHUNK - 1, 0), 1), :]
    prev = jnp.where(j == 0, -1, prev)
    last = segc_ref[pl.ds(j * CHUNK + CHUNK - 1, 1), :]
    valid = lanes(CHUNK) < CHIP_HEADS
    raw = proj_ref[rows, T0 : T0 + 128].astype(F32) + par_ref[0:1, :]
    dt = jnp.where(valid, jnp.maximum(raw, 0.0) + jnp.log1p(jnp.exp(-jnp.abs(raw))), 0.0)
    decay = dt * par_ref[1:2, :]
    place = lax.broadcasted_iota(jnp.int32, (CHUNK, CHUNK), 0)
    under = (place >= lanes(CHUNK, CHUNK)).astype(F32)
    cum = dot(under, decay, precision=lax.Precision.HIGHEST)
    end = cum[CHUNK - 1 : CHUNK, :]
    from_start = jnp.where(seg == prev, jnp.exp(cum), 0.0)
    to_end = jnp.where(seg == last, jnp.exp(end - cum), 0.0)
    keep = jnp.where(last == prev, jnp.exp(end), 0.0)
    return rows, raw, dt, decay, cum, from_start, to_end, keep, under


def scan_forward(proj_ref, segc_ref, segr_ref, par_ref, spread_ref, wide_ref, gated_ref, y_ref, states_ref, state):
    spread = spread_ref[...]
    state[...] = jnp.zeros_like(state)

    def chunk(j, carry):
        rows, raw, dt, decay, cum, from_start, to_end, keep, under = scan_pieces(j, proj_ref, segc_ref, segr_ref, par_ref)
        place = lax.broadcasted_iota(jnp.int32, (CHUNK, CHUNK), 0)
        same = segc_ref[rows, 0:1] == segr_ref[0:1, rows]
        mask = jnp.where(same & (place >= lanes(CHUNK, CHUNK)), 0.0, FAR)
        cum_t = cum.T
        b = proj_ref[rows, B0 : B0 + 128]
        c = proj_ref[rows, C0 : C0 + 128]
        cb = dot(c, b, ((1,), (1,)))
        x = proj_ref[rows, X0 : X0 + XW].astype(F32)
        xdt = x * widen(dt, spread)
        xdt_low = xdt.astype(BF)
        old = state[...]
        states_ref[j] = old
        y_state = dot(c, old.astype(BF)) * widen(from_start, spread)
        low = lanes(CHUNK) < 64
        for pair in range(CHIP_HEADS // 2):
            cols = slice(128 * pair, 128 * (pair + 1))
            xp = xdt_low[:, cols]
            local = y_state[:, cols]
            for half in range(2):
                h = 2 * pair + half
                spread_h = jnp.exp(cum[:, h : h + 1] - cum_t[h : h + 1, :] + mask)
                mix = (cb * spread_h).astype(BF)
                xh = jnp.where(low if half == 0 else ~low, xp, jnp.zeros_like(xp))
                local = local + dot(mix, xh)
            y_ref[rows, cols] = local
            y = (local + x[:, cols] * wide_ref[0:1, cols]).astype(BF).astype(F32)
            z = proj_ref[rows, Z0 + 128 * pair : Z0 + 128 * (pair + 1)].astype(F32)
            gated_ref[rows, cols] = (y * (z / (1.0 + jnp.exp(-z)))).astype(BF)
        weighted = (xdt * widen(to_end, spread)).astype(BF)
        keep_wide = widen(jnp.broadcast_to(keep, (8, 128)), spread)[0:1, :]
        state[...] = old * keep_wide + dot(b, weighted, ((0,), (0,)))
        return carry

    lax.fori_loop(0, proj_ref.shape[0] // CHUNK, chunk, 0)


def scan_backward(proj_ref, segc_ref, segr_ref, par_ref, spread_ref, wide_ref, y_ref, states_ref, ggated_ref, gproj_ref, gpar_ref, gstate):
    spread = spread_ref[...]
    gstate[...] = jnp.zeros_like(gstate)
    gpar_ref[...] = jnp.zeros_like(gpar_ref)
    chunks = proj_ref.shape[0] // CHUNK

    def narrow(v):
        top = v.astype(BF)
        rest = (v - top.astype(F32)).astype(BF)
        return dot(top, spread, ((1,), (1,))) + dot(rest, spread, ((1,), (1,)))

    def chunk(step, carry):
        j = chunks - 1 - step
        rows, raw, dt, decay, cum, from_start, to_end, keep, under = scan_pieces(j, proj_ref, segc_ref, segr_ref, par_ref)
        place = lax.broadcasted_iota(jnp.int32, (CHUNK, CHUNK), 0)
        same = segc_ref[rows, 0:1] == segr_ref[0:1, rows]
        mask = jnp.where(same & (place <= lanes(CHUNK, CHUNK)), 0.0, FAR)
        cum_t = cum.T
        b = proj_ref[rows, B0 : B0 + 128]
        c = proj_ref[rows, C0 : C0 + 128]
        bc = dot(b, c, ((1,), (1,)))
        x = proj_ref[rows, X0 : X0 + XW].astype(F32)
        dt_wide = widen(dt, spread)
        xdt_low = (x * dt_wide).astype(BF)
        start_wide = widen(from_start, spread)
        end_wide = widen(to_end, spread)
        old = states_ref[j]
        gnew = gstate[...]
        z = proj_ref[rows, Z0 : Z0 + XW].astype(F32)
        gg = ggated_ref[rows, :].astype(F32)
        y_own = y_ref[rows, :]
        y = (y_own + x * wide_ref[0:1, :]).astype(BF).astype(F32)
        sig = 1.0 / (1.0 + jnp.exp(-z))
        gy_low = (gg * (z * sig)).astype(BF)
        gproj_ref[rows, Z0 : Z0 + XW] = (gg * y * (sig * (1.0 + z * (1.0 - sig)))).astype(BF)
        gy = gy_low.astype(F32)
        gx_state = end_wide * dot(b, gnew.astype(BF))
        gbc = jnp.zeros((CHUNK, CHUNK), F32)
        low = lanes(CHUNK) < 64
        gxdt = []
        for pair in range(CHIP_HEADS // 2):
            cols = slice(128 * pair, 128 * (pair + 1))
            xp, gp = xdt_low[:, cols], gy_low[:, cols]
            total = gx_state[:, cols]
            for half in range(2):
                h = 2 * pair + half
                mine = low if half == 0 else ~low
                spread_h = jnp.exp(cum_t[h : h + 1, :] - cum[:, h : h + 1] + mask)
                mix = (bc * spread_h).astype(BF)
                gh = jnp.where(mine, gp, jnp.zeros_like(gp))
                total = total + dot(mix, gh)
                gbc = gbc + dot(xp, gh, ((1,), (1,))) * spread_h
            gxdt.append(total)
        gxdt = jnp.concatenate(gxdt, axis=1)
        gstart = (gy * start_wide).astype(BF)
        weighted = (xdt_low.astype(F32) * end_wide).astype(BF)
        gbc_low = gbc.astype(BF)
        gnew_low, old_low = gnew.astype(BF), old.astype(BF)
        gproj_ref[rows, C0 : C0 + 128] = (dot(gbc_low, b, ((0,), (0,))) + dot(gstart, old_low, ((1,), (1,)))).astype(BF)
        gproj_ref[rows, B0 : B0 + 128] = (dot(gbc_low, c) + dot(weighted, gnew_low, ((1,), (1,)))).astype(BF)
        keep_wide = widen(jnp.broadcast_to(keep, (8, 128)), spread)[0:1, :]
        kept = jnp.sum(old * gnew, axis=0, keepdims=True) * keep_wide
        gstate[...] = gnew * keep_wide + dot(c, gstart, ((0,), (0,)))
        xdt_f = xdt_low.astype(F32)
        gcum = narrow(gy * y_own) - narrow(xdt_f * gxdt)
        at_end = jnp.sum(xdt_f * gx_state, axis=0, keepdims=True) + kept
        at_end = narrow(jnp.broadcast_to(at_end, (8, XW)))[0:1, :]
        gdecay = dot(under, gcum, ((0,), (0,)), precision=lax.Precision.HIGHEST) + at_end
        gdt = narrow(gxdt * x) + gdecay * par_ref[1:2, :]
        graw = gdt / (1.0 + jnp.exp(-raw))
        graw = jnp.where(lanes(CHUNK) < CHIP_HEADS, graw, 0.0)
        gproj_ref[rows, T0 : T0 + 128] = graw.astype(BF)
        gproj_ref[rows, X0 : X0 + XW] = (gxdt * dt_wide + gy * wide_ref[0:1, :]).astype(BF)
        gpar_ref[0:1, :] += jnp.sum(graw, axis=0, keepdims=True)
        gpar_ref[1:2, :] += jnp.sum(gdecay * decay, axis=0, keepdims=True)
        skip = jnp.sum(gy * x, axis=0, keepdims=True)
        gpar_ref[2:3, :] += narrow(jnp.broadcast_to(skip, (8, XW)))[0:1, :]
        return carry

    lax.fori_loop(0, chunks, chunk, 0)


def forward_kernel(proj, cosine, sine, segc, segr, par, spread, wide, gated, attn, lse, y, states, state):
    attention_forward(proj, cosine, sine, segc, segr, attn, lse)
    scan_forward(proj, segc, segr, par, spread, wide, gated, y, states, state)


def backward_kernel(proj, cosine, sine, segc, segr, par, spread, wide, attn, lse, y, states, ggated, gattn, gproj, gpar, gkv, gstate):
    attention_backward(proj, cosine, sine, segc, segr, attn, lse, gattn, gproj, gkv)
    scan_backward(proj, segc, segr, par, spread, wide, y, states, ggated, gproj, gpar, gstate)


def whole(n):
    return [pl.BlockSpec(memory_space=VM)] * n


def mixer_forward(proj, consts):
    seq_len = proj.shape[0]
    chunks = seq_len // CHUNK
    return pl.pallas_call(
        forward_kernel,
        name="mixer_forward",
        out_shape=(
            jax.ShapeDtypeStruct((seq_len, XW), BF),
            jax.ShapeDtypeStruct((seq_len, QW), BF),
            jax.ShapeDtypeStruct((seq_len, 128), F32),
            jax.ShapeDtypeStruct((seq_len, XW), F32),
            jax.ShapeDtypeStruct((chunks, NS, XW), F32),
        ),
        in_specs=whole(8),
        out_specs=tuple(whole(5)),
        scratch_shapes=[VM((NS, XW), F32)],
        compiler_params=pltpu.CompilerParams(vmem_limit_bytes=56 * MIB),
    )(proj, *consts)


def mixer_backward(proj, consts, attn, lse, y, states, ggated, gattn):
    seq_len = proj.shape[0]
    return pl.pallas_call(
        backward_kernel,
        name="mixer_backward",
        out_shape=(
            jax.ShapeDtypeStruct((seq_len, COLS), BF),
            jax.ShapeDtypeStruct((8, 128), F32),
        ),
        in_specs=whole(14),
        out_specs=tuple(whole(2)),
        scratch_shapes=[VM((seq_len, 256), F32), VM((NS, XW), F32)],
        compiler_params=pltpu.CompilerParams(vmem_limit_bytes=56 * MIB),
    )(proj, *consts, attn, lse, y, states, ggated, gattn)


def place():
    d, s = lax.axis_index("dp"), lax.axis_index("seq")
    return d // 2, d % 2, s // 2, s % 2


def device(z, x, y, c):
    return (2 * z + x, 2 * y + c)


def greet(peers):
    barrier = pltpu.get_barrier_semaphore()
    for peer in peers:
        pl.semaphore_signal(barrier, inc=1, device_id=peer, device_id_type=MESH)
    pl.semaphore_wait(barrier, len(peers))


def send(src, dst, sems, k, target):
    copy = pltpu.make_async_remote_copy(
        src_ref=src, dst_ref=dst, send_sem=sems[0].at[k], recv_sem=sems[1].at[k], device_id=target, device_id_type=MESH
    )
    copy.start()
    return copy


def landed(dst, sems, k, target):
    pltpu.make_async_remote_copy(
        src_ref=dst, dst_ref=dst, send_sem=sems[0].at[k], recv_sem=sems[1].at[k], device_id=target, device_id_type=MESH
    ).wait_recv()


ARRAY_SENDS = 13


class Gather:
    def __init__(self, src, dst, sems, base, local_sem):
        self.src, self.dst, self.sems, self.base = src, dst, sems, base
        self.local_sem = local_sem
        self.z, self.x, self.y, self.c = place()
        half = src.shape[0] // 2
        self.mine = pl.ds(self.y * half, half)
        self.other = pl.ds((1 - self.y) * half, half)
        self.sent = []
        self.xpeer = device(self.z, 1 - self.x, self.y, self.c)
        self.ypeer = device(self.z, self.x, 1 - self.y, self.c)

    def block(self, r, x, rows):
        return self.dst.at[2 * (self.z ^ r) + x, rows]

    def push(self, k, ref, target, dst=None):
        self.sent.append(send(ref, ref if dst is None else dst, self.sems, self.base + k, target))

    def start(self):
        own = 2 * self.z + self.x
        self.local = pltpu.make_async_copy(self.src, self.dst.at[own], self.local_sem)
        self.local.start()
        for r in (1, 2, 3):
            target = device(self.z ^ r, self.x, self.y, self.c)
            self.push(r - 1, self.src.at[self.mine], target, self.dst.at[own, self.mine])
        self.push(3, self.src, self.xpeer, self.dst.at[own])

    def forward(self, r):
        ref = self.block(r, self.x, self.mine)
        landed(ref, self.sems, self.base + r - 1, self.xpeer)
        self.push(3 + r, ref, self.xpeer)
        self.push(6 + r, ref, self.ypeer)

    def corner(self, r):
        if r == 1:
            ref = self.block(r, self.x, self.other)
            landed(ref, self.sems, self.base + 6 + r, self.ypeer)
            self.push(9 + r, ref, self.xpeer)
        else:
            ref = self.block(r, 1 - self.x, self.mine)
            landed(ref, self.sems, self.base + 3 + r, self.xpeer)
            self.push(9 + r, ref, self.ypeer)

    def finish(self):
        landed(self.dst.at[2 * self.z + 1 - self.x], self.sems, self.base + 3, self.xpeer)
        for r in (1, 2, 3):
            if r == 1:
                landed(self.block(r, 1 - self.x, self.mine), self.sems, self.base + 3 + r, self.xpeer)
            else:
                landed(self.block(r, self.x, self.other), self.sems, self.base + 6 + r, self.ypeer)
            landed(self.block(r, 1 - self.x, self.other), self.sems, self.base + 9 + r, self.ypeer)
        for copy in self.sent:
            copy.wait_send()
        self.local.wait()


def chip_peers():
    z, x, y, c = place()
    peers = [device(z ^ r, x, y, c) for r in (1, 2, 3)]
    peers += [device(z, 1 - x, y, c), device(z, x, 1 - y, c), device(z, x, y, 1 - c)]
    return peers


def start_kernel(dealt, cot, w, rows, weights, gcot, dsend, drecv, wsend, wrecv, local):
    z, x, y, c = place()
    own = 2 * z + x
    slot = 2 * y + c
    partner = device(z, x, y, 1 - c)
    ypeer = device(z, x, 1 - y, c)
    others = [(r, i, j) for r in range(4) for i in range(2) for j in range(2) if r or i or j]
    targets = [device(z ^ r, x ^ i, y ^ j, c) for r, i, j in others]
    greet(targets + [partner])
    sems = (dsend, drecv)
    gather = Gather(w, weights, (wsend, wrecv), 0, local.at[0])
    columns = lambda d: pl.ds(pl.multiple_of(d * 128, 128), 128)
    sent = []
    for k, (r, i, j) in enumerate(others):
        pack = 2 * (2 * (z ^ r) + (x ^ i)) + (y ^ j)
        sent.append(send(dealt.at[pack], rows.at[slot, :, columns(own)], sems, k, targets[k]))
    here = pltpu.make_async_copy(dealt.at[2 * own + y], rows.at[slot, :, columns(own)], local.at[1])
    here.start()
    gather.start()
    sent.append(send(cot.at[1 - y], gcot.at[slot], sems, 18, ypeer))
    sent.append(send(cot.at[y], gcot.at[slot], sems, 19, partner))
    mine = pltpu.make_async_copy(cot.at[y], gcot.at[slot], local.at[2])
    mine.start()
    for r in (1, 2, 3):
        gather.forward(r)
    here.wait()
    for same_y in (True, False):
        for k, (r, i, j) in enumerate(others):
            if (j == 0) == same_y:
                src = 2 * (z ^ r) + (x ^ i)
                landed(rows.at[2 * (y ^ j) + c, :, columns(src)], sems, k, targets[k])
        ref = rows.at[slot if same_y else 2 * (1 - y) + c]
        sent.append(send(ref, ref, sems, 15 if same_y else 16, partner))
    for r in (1, 2, 3):
        gather.corner(r)
    ref = gcot.at[2 * (1 - y) + c]
    landed(ref, sems, 18, ypeer)
    sent.append(send(ref, ref, sems, 17, partner))
    landed(rows.at[2 * y + 1 - c], sems, 15, partner)
    landed(rows.at[2 * (1 - y) + 1 - c], sems, 16, partner)
    landed(gcot.at[2 * (1 - y) + 1 - c], sems, 17, partner)
    landed(gcot.at[2 * y + 1 - c], sems, 19, partner)
    for copy in sent:
        copy.wait_send()
    gather.finish()
    mine.wait()


def any_specs(n):
    return [pl.BlockSpec(memory_space=pl.ANY)] * n


def start_transfers(dealt, cot, w):
    packs, span, width = dealt.shape
    return pl.pallas_call(
        start_kernel,
        name="deal_and_gather",
        out_shape=(
            jax.ShapeDtypeStruct((4, span, 8 * width), BF),
            jax.ShapeDtypeStruct((8,) + w.shape, BF),
            jax.ShapeDtypeStruct((4,) + cot.shape[1:], BF),
        ),
        in_specs=any_specs(3),
        out_specs=tuple(any_specs(3)),
        scratch_shapes=[
            pltpu.SemaphoreType.DMA((20,)),
            pltpu.SemaphoreType.DMA((20,)),
            pltpu.SemaphoreType.DMA((ARRAY_SENDS,)),
            pltpu.SemaphoreType.DMA((ARRAY_SENDS,)),
            pltpu.SemaphoreType.DMA((3,)),
        ],
        compiler_params=pltpu.CompilerParams(collective_id=0, has_side_effects=True),
    )(dealt, cot, w)


def gather_kernel(ssm, att, gu, dn, ssm_own, att_own, gu_all, dn_all, ssm_all, att_all, gsend, grecv, csend, crecv, local):
    z, x, y, c = place()
    partner = device(z, x, y, 1 - c)
    greet(chip_peers())
    sems = (gsend, grecv)
    pairs = ((ssm, ssm_all), (att, att_all), (gu, gu_all), (dn, dn_all))
    gathers = [Gather(a, b, sems, ARRAY_SENDS * i, local.at[i]) for i, (a, b) in enumerate(pairs)]
    for g in gathers:
        g.start()
    for g in gathers:
        for r in (1, 2, 3):
            g.forward(r)
    for g in gathers:
        for r in (1, 2, 3):
            g.corner(r)
    sent = []
    for i, (g, out) in enumerate(zip(gathers[:2], (ssm_own, att_own))):
        g.finish()
        half = g.src.shape[1]
        columns = lambda k: pl.ds(pl.multiple_of(k * half, 128), half)
        here = pltpu.make_async_copy(g.dst.at[pl.ds(4 * c, 4)], out.at[:, :, columns(c)], local.at[4 + i])
        here.start()
        sent.append(here)
        sent.append(send(g.dst.at[pl.ds(4 * (1 - c), 4)], out.at[:, :, columns(c)], (csend, crecv), i, partner))
    for g in gathers[2:]:
        g.finish()
    for i, out in enumerate((ssm_own, att_own)):
        half = out.shape[2] // 2
        landed(out.at[:, :, pl.ds(pl.multiple_of((1 - c) * half, 128), half)], (csend, crecv), i, partner)
        sent[2 * i].wait()
        sent[2 * i + 1].wait_send()


def gather_weights(ssm, att, gu, dn):
    total = 4 * ARRAY_SENDS
    outs = pl.pallas_call(
        gather_kernel,
        name="gather_weights",
        out_shape=(
            jax.ShapeDtypeStruct((4, ssm.shape[0], 2 * ssm.shape[1]), BF),
            jax.ShapeDtypeStruct((4, att.shape[0], 2 * att.shape[1]), BF),
            jax.ShapeDtypeStruct((8,) + gu.shape, BF),
            jax.ShapeDtypeStruct((8,) + dn.shape, BF),
            jax.ShapeDtypeStruct((8,) + ssm.shape, BF),
            jax.ShapeDtypeStruct((8,) + att.shape, BF),
        ),
        in_specs=any_specs(4),
        out_specs=tuple(any_specs(6)),
        scratch_shapes=[
            pltpu.SemaphoreType.DMA((total,)),
            pltpu.SemaphoreType.DMA((total,)),
            pltpu.SemaphoreType.DMA((2,)),
            pltpu.SemaphoreType.DMA((2,)),
            pltpu.SemaphoreType.DMA((6,)),
        ],
        compiler_params=pltpu.CompilerParams(collective_id=1, has_side_effects=True),
    )(ssm, att, gu, dn)
    return [v.reshape(-1, v.shape[-1]) for v in outs[:4]]


def pair_kernel(blocks, part, got, sems_out, sems_in):
    z, x, y, c = place()
    partner = device(z, x, y, 1 - c)
    greet([partner])
    sems = (sems_out, sems_in)
    if blocks:
        sent = [send(part.at[2 * k + 1 - c], got.at[k], sems, k, partner) for k in range(2)]
    else:
        sent = [send(part, got, sems, 0, partner)]
    for copy in sent:
        copy.wait()


def pair_swap(part):
    blocks = part.ndim == 3
    return pl.pallas_call(
        functools.partial(pair_kernel, blocks),
        name="pair_swap_rows" if blocks else "pair_swap",
        out_shape=jax.ShapeDtypeStruct(((2,) + part.shape[1:]) if blocks else part.shape, BF),
        in_specs=any_specs(1),
        out_specs=any_specs(1)[0],
        scratch_shapes=[pltpu.SemaphoreType.DMA((2,)), pltpu.SemaphoreType.DMA((2,))],
        compiler_params=pltpu.CompilerParams(collective_id=3 if blocks else 2, has_side_effects=True),
    )(part)


def columns_kernel(ssm, att, ssm_all, att_all, sems_out, sems_in, local):
    z, x, y, c = place()
    partner = device(z, x, y, 1 - c)
    greet([partner])
    copies = []
    for i, (src, dst) in enumerate(((ssm, ssm_all), (att, att_all))):
        half = src.shape[2] // 2
        columns = lambda k: src.at[:, :, pl.ds(pl.multiple_of(k * half, 128), half)]
        here = pltpu.make_async_copy(columns(c), dst.at[pl.ds(4 * c, 4)], local.at[i])
        here.start()
        copies += [here, send(columns(1 - c), dst.at[pl.ds(4 * c, 4)], (sems_out, sems_in), i, partner)]
    for i, dst in enumerate((ssm_all, att_all)):
        copies[2 * i].wait()
        copies[2 * i + 1].wait_send()
        landed(dst.at[pl.ds(4 * (1 - c), 4)], (sems_out, sems_in), i, partner)


def swap_columns(ssm, att):
    args = [v.reshape(4, -1, v.shape[-1]) for v in (ssm, att)]
    return pl.pallas_call(
        columns_kernel,
        name="swap_columns",
        out_shape=tuple(jax.ShapeDtypeStruct((8, v.shape[1], v.shape[2] // 2), BF) for v in args),
        in_specs=any_specs(2),
        out_specs=tuple(any_specs(2)),
        scratch_shapes=[pltpu.SemaphoreType.DMA((2,))] * 3,
        compiler_params=pltpu.CompilerParams(collective_id=5, has_side_effects=True),
    )(*args)


class Reduce:
    VIA_X = (0, 1)

    def __init__(self, part, out, far, near_x, near_y, deep, sems, base):
        self.part, self.out, self.far, self.near_x, self.near_y, self.deep = part, out, far, near_x, near_y, deep
        self.sems, self.base = sems, base
        self.z, self.x, self.y, self.c = place()
        half = part.shape[1] // 2
        self.mine = pl.ds(self.y * half, half)
        self.other = pl.ds((1 - self.y) * half, half)
        self.xpeer = device(self.z, 1 - self.x, self.y, self.c)
        self.ypeer = device(self.z, self.x, 1 - self.y, self.c)
        self.sent = []

    def piece(self, r, x, rows):
        return self.part.at[2 * (self.z ^ r) + x, rows]

    def push(self, k, src, dst, target):
        self.sent.append(send(src, dst, self.sems, self.base + k, target))

    def start(self):
        for r in (1, 2, 3, 0):
            far = self.piece(r, 1 - self.x, self.other)
            self.push(r, far, self.far.at[r], self.xpeer if r in self.VIA_X else self.ypeer)
        for r in (1, 2, 3, 0):
            if r in self.VIA_X:
                self.push(4 + r, self.piece(r, 1 - self.x, self.mine), self.near_x.at[r], self.xpeer)
            else:
                self.push(8 + r, self.piece(r, self.x, self.other), self.near_y.at[r], self.ypeer)

    def relay(self, r):
        landed(self.far.at[r], self.sems, self.base + r, self.xpeer)
        own = self.piece(r, self.x, self.other) if r in self.VIA_X else self.piece(r, 1 - self.x, self.mine)
        self.far[r] = (own[...].astype(F32) + self.far[r].astype(F32)).astype(BF)
        if r in self.VIA_X:
            self.push(8 + r, self.far.at[r], self.near_y.at[r], self.ypeer)
        else:
            self.push(4 + r, self.far.at[r], self.near_x.at[r], self.xpeer)

    def root(self, r):
        landed(self.near_x.at[r], self.sems, self.base + 4 + r, self.xpeer)
        landed(self.near_y.at[r], self.sems, self.base + 8 + r, self.ypeer)
        own = self.piece(r, self.x, self.mine)[...].astype(F32)
        total = own + (self.near_x[r].astype(F32) + self.near_y[r].astype(F32))
        self.near_x[r] = total.astype(BF)
        if r:
            target = device(self.z ^ r, self.x, self.y, self.c)
            self.push(11 + r, self.near_x.at[r], self.deep.at[r - 1], target)

    def total(self, partner):
        for r in (1, 2, 3):
            landed(self.deep.at[r - 1], self.sems, self.base + 11 + r, self.xpeer)
        total = self.near_x[0].astype(F32) + self.deep[0].astype(F32)
        total = total + (self.deep[1].astype(F32) + self.deep[2].astype(F32))
        self.out[self.c, self.mine] = total.astype(BF)
        ref = self.out.at[self.c, self.mine]
        self.push(15, ref, ref, self.ypeer)
        self.push(16, ref, ref, partner)

    def spread(self, partner):
        ref = self.out.at[self.c, self.other]
        landed(ref, self.sems, self.base + 15, self.ypeer)
        self.push(17, ref, ref, partner)

    def finish(self, partner):
        landed(self.out.at[1 - self.c, self.mine], self.sems, self.base + 16, partner)
        landed(self.out.at[1 - self.c, self.other], self.sems, self.base + 17, partner)
        for copy in self.sent:
            copy.wait_send()


REDUCE_SENDS = 18
N_REDUCED = 5


def reduce_kernel(*refs):
    parts, refs = refs[:N_REDUCED], refs[N_REDUCED:]
    out_rows, gx, refs = refs[0], refs[1], refs[2:]
    reduced, refs = refs[:N_REDUCED], refs[N_REDUCED:]
    output, returned, refs = refs[0], refs[1], refs[2:]
    buffers, refs = [refs[4 * i : 4 * i + 4] for i in range(N_REDUCED)], refs[4 * N_REDUCED :]
    rsend, rrecv, dsend, drecv, local = refs
    z, x, y, c = place()
    own = 2 * z + x
    slot = 2 * own + y
    partner = device(z, x, y, 1 - c)
    ypeer = device(z, x, 1 - y, c)
    others = [(r, i, j) for r in range(4) for i in range(2) for j in range(2) if r or i or j]
    targets = [device(z ^ r, x ^ i, y ^ j, c) for r, i, j in others]
    greet(targets + [partner])
    sums = [Reduce(p, o, *b, (rsend, rrecv), REDUCE_SENDS * k) for k, (p, o, b) in enumerate(zip(parts, reduced, buffers))]
    for s in sums:
        s.start()
    columns = lambda d: pl.ds(pl.multiple_of(d * 128, 128), 128)
    sems = (dsend, drecv)
    sent = [send(out_rows.at[1 - y], output.at[y], sems, 15, ypeer)]
    here = [
        pltpu.make_async_copy(out_rows.at[y], output.at[y], local.at[0]),
        pltpu.make_async_copy(gx.at[y, :, columns(own)], returned.at[slot], local.at[1]),
    ]
    for copy in here:
        copy.start()
    for k, (r, i, j) in enumerate(others):
        d = 2 * (z ^ r) + (x ^ i)
        sent.append(send(gx.at[y ^ j, :, columns(d)], returned.at[slot], sems, k, targets[k]))
    for s in sums:
        for r in (1, 2, 3, 0):
            s.relay(r)
    for s in sums:
        for r in (1, 2, 3, 0):
            s.root(r)
    for s in sums:
        s.total(partner)
    for s in sums:
        s.spread(partner)
    for s in sums:
        s.finish(partner)
    for k, (r, i, j) in enumerate(others):
        landed(returned.at[2 * (2 * (z ^ r) + (x ^ i)) + (y ^ j)], sems, k, targets[k])
    landed(output.at[1 - y], sems, 15, ypeer)
    for copy in sent:
        copy.wait_send()
    for copy in here:
        copy.wait()


def reduce_all(parts, out_rows, gx):
    outs = [jax.ShapeDtypeStruct((2,) + p.shape[1:], BF) for p in parts]
    outs += [jax.ShapeDtypeStruct(out_rows.shape, BF), jax.ShapeDtypeStruct((16, gx.shape[1], 128), BF)]
    scratch = []
    for p in parts:
        half = (p.shape[1] // 2, p.shape[2])
        scratch += [VM((4,) + half, BF)] * 3 + [VM((3,) + half, BF)]
    total = REDUCE_SENDS * len(parts)
    scratch += [pltpu.SemaphoreType.DMA((n,)) for n in (total, total, 16, 16, 2)]
    return pl.pallas_call(
        reduce_kernel,
        name="reduce_and_return",
        out_shape=tuple(outs),
        in_specs=whole(len(parts)) + any_specs(2),
        out_specs=tuple(whole(len(parts)) + any_specs(2)),
        scratch_shapes=scratch,
        compiler_params=pltpu.CompilerParams(collective_id=4, has_side_effects=True, vmem_limit_bytes=60 * MIB),
    )(*parts, out_rows, gx)


def plain_start(dealt, cot, w, y):
    arrived = lax.all_to_all(dealt, "dp", split_axis=0, concat_axis=2, tiled=True)
    rows = lax.all_gather(arrived, "seq", axis=1, tiled=True)
    cots = lax.all_gather(cot, "seq", axis=1, tiled=True)
    pick = lambda v: lax.dynamic_index_in_dim(v, y, 0, keepdims=False)
    return pick(rows), lax.all_gather(w, "dp", axis=0, tiled=True), pick(cots)


def plain_gather(ssm, att, gu, dn, c):
    every = [lax.all_gather(v, "dp", axis=0, tiled=True) for v in (ssm, att, gu, dn)]
    out = []
    for v in every[:2]:
        rows = v.shape[0] // 2
        mine = lax.all_gather(v, "seq", axis=1, tiled=True)[:, : 2 * v.shape[1]]
        out.append(lax.dynamic_slice_in_dim(mine, c * rows, rows))
    return out + every[2:]


def plain_pair(part):
    return lax.ppermute(part, "seq", [(0, 1), (1, 0), (2, 3), (3, 2)])


def plain_reduce(parts, out_rows, gx, y, c):
    reduced = []
    for p in parts:
        total = lax.psum_scatter(p.reshape(-1, p.shape[-1]), "dp", scatter_dimension=0, tiled=True)
        every = lax.all_gather(total, "seq", axis=0).astype(F32)
        reduced.append(jnp.stack([every[0] + every[2], every[1] + every[3]]))
    peer = lax.ppermute(out_rows, "seq", [(0, 2), (1, 3), (2, 0), (3, 1)])
    output = jnp.where(jnp.arange(2)[:, None, None] == y, out_rows, jnp.flip(peer, 0))
    whole_rows = lax.all_gather(gx, "seq", axis=0)
    slot = 2 * y + c
    by_pack = lax.dynamic_index_in_dim(whole_rows, c, 0, False), lax.dynamic_index_in_dim(whole_rows, c + 2, 0, False)
    both = jnp.stack([lax.dynamic_index_in_dim(v, y, 0, False) for v in by_pack])
    returned = lax.all_to_all(both, "dp", split_axis=2, concat_axis=0, tiled=True)
    return reduced, output, returned


def rms_parts(v):
    scale = lax.rsqrt(jnp.mean(v * v, axis=-1, keepdims=True) + EPS)
    return v * scale, scale


def rms_back(normed, scale, gain, grad):
    inner = grad * gain
    return scale * (inner - normed * jnp.mean(inner * normed, axis=-1, keepdims=True))


def silu(v):
    return v / (1.0 + jnp.exp(-v))


def low(v):
    return v.astype(BF)


def body(tokens, cot, seq_lengths, deal_order, in_gain, in_proj, dt_proj, dt_bias, a_log, d_skip, ssm_out, attn_out, ffn_gain, gate_up, down_proj):
    groups = lax.axis_size("dp")
    fast = groups == 8
    dp_index, seq_index = lax.axis_index("dp"), lax.axis_index("seq")
    y, c = seq_index // 2, seq_index % 2
    packs, span, width = cot.shape
    seq_len = span * lax.axis_size("seq")
    inner = MH * HP
    block = in_proj.shape[0]

    cut = lambda v, start, size: lax.dynamic_slice_in_dim(v, start, size, axis=1)
    q_start = 2 * inner + 2 * NS
    k_start = q_start + QUERY_HEADS * HEAD_WIDTH
    v_start = k_start + KEY_VALUE_HEADS * HEAD_WIDTH
    w_in = jnp.concatenate(
        [
            cut(in_proj, XW * c, XW),
            cut(in_proj, inner + XW * c, XW),
            cut(in_proj, q_start + QW * c, QW),
            cut(in_proj, k_start + HEAD_WIDTH * c, HEAD_WIDTH),
            cut(in_proj, v_start + HEAD_WIDTH * c, HEAD_WIDTH),
            in_proj[:, 2 * inner : q_start],
            cut(dt_proj, CHIP_HEADS * c, CHIP_HEADS),
            in_gain[:, None],
            ffn_gain[:, None],
            jnp.zeros((block, 128 - CHIP_HEADS - 2), BF),
        ],
        axis=1,
    )
    half_units = down_proj.shape[0] // 2
    w_gu = gate_up.reshape(block, 2, groups, 2, half_units)
    w_gu = lax.dynamic_index_in_dim(w_gu, c, 3, keepdims=False).reshape(block, FF)
    w_dn = lax.dynamic_slice_in_dim(down_proj, half_units * c, half_units, axis=0)
    w_ssm = cut(ssm_out, width // 2 * c, width // 2)
    w_att = cut(attn_out, width // 2 * c, width // 2)

    dealt = jnp.take(tokens, deal_order, axis=0)
    if fast:
        rows, w_in, cots = start_transfers(dealt, cot, w_in)
        rows, cots = rows.reshape(seq_len, width), cots.reshape(seq_len, width)
        w_in = w_in.reshape(width, COLS)
        w_ssm, w_att, w_gu, w_dn = gather_weights(w_ssm, w_att, w_gu, w_dn)
        pair = pair_swap
    else:
        rows, w_in, cots = plain_start(dealt, cot, w_in, y)
        w_ssm, w_att, w_gu, w_dn = plain_gather(w_ssm, w_att, w_gu, w_dn, c)
        pair = plain_pair

    pack = lax.dynamic_index_in_dim(deal_order, dp_index * packs + y, 0, keepdims=False)
    ends = jnp.cumsum(lax.dynamic_index_in_dim(seq_lengths, pack, 0, keepdims=False))[:-1]
    places = jnp.arange(seq_len, dtype=jnp.int32)
    seg = jnp.sum((places[:, None] >= ends[None, :]).astype(jnp.int32), axis=1)
    segc = jnp.broadcast_to(seg[:, None], (seq_len, 128))
    segr = jnp.broadcast_to(seg[None, :], (8, seq_len))
    half = HEAD_WIDTH // 2
    frequency = THETA ** (-jnp.arange(half, dtype=F32) * 2.0 / HEAD_WIDTH)
    angles = places.astype(F32)[:, None] * frequency[None, :]
    cosine = jnp.tile(jnp.cos(angles), (1, 4))
    sine = jnp.tile(jnp.concatenate([-jnp.sin(angles), jnp.sin(angles)], axis=1), (1, 2))
    own_heads = lambda v: lax.dynamic_slice_in_dim(v, CHIP_HEADS * c, CHIP_HEADS)
    par = jnp.zeros((8, 128), F32)
    par = par.at[0, :CHIP_HEADS].set(own_heads(dt_bias)).at[1, :CHIP_HEADS].set(-jnp.exp(own_heads(a_log)))
    wide = jnp.broadcast_to(jnp.repeat(own_heads(d_skip), HP)[None, :], (8, XW))
    head_of = jnp.arange(XW) // HP
    spread = (jnp.arange(128)[:, None] % 64 == head_of[None, :]).astype(BF)
    consts = (cosine, sine, segc, segr, par, spread, wide)

    x = rows.astype(F32)
    gain_in = w_in[:, T0 + CHIP_HEADS].astype(F32)[None, :]
    gain_ffn = w_in[:, T0 + CHIP_HEADS + 1].astype(F32)[None, :]
    unit_in, scale_in = rms_parts(x)
    normed = low(unit_in * gain_in)
    proj = low(dot(normed, w_in))
    gated, attn, lse, y_own, states = mixer_forward(proj, consts)
    part = low(dot(gated, w_ssm) + dot(attn, w_att))
    middle = x + (part.astype(F32) + pair(part).astype(F32))
    unit_ffn, scale_ffn = rms_parts(middle)
    normed_two = low(unit_ffn * gain_ffn)
    gu = low(dot(normed_two, w_gu)).astype(F32)
    gate, up = gu[:, : FF // 2], gu[:, FF // 2 :]
    act = low(silu(gate) * up)
    out_part = low(dot(act, w_dn)).reshape(4, span, width)
    by_core = lambda v: lax.dynamic_index_in_dim(v.reshape(2, 2, span, width), c, 1, keepdims=False)
    swap_rows = (lambda v: pair(v)) if fast else (lambda v: by_core(plain_pair(v)))
    out_rows = low(by_core(middle) + (by_core(out_part).astype(F32) + swap_rows(out_part).astype(F32)))

    g_act = low(dot(cots, w_dn, ((1,), (1,)))).astype(F32)
    grad_dn = low(dot(act, cots, ((0,), (0,))))
    sig = 1.0 / (1.0 + jnp.exp(-gate))
    g_gu = low(jnp.concatenate([g_act * up * (sig * (1.0 + gate * (1.0 - sig))), g_act * (gate * sig)], axis=1))
    grad_gu = low(dot(normed_two, g_gu, ((0,), (0,))))
    part = low(dot(g_gu, w_gu, ((1,), (1,))))
    g_two = low(part.astype(F32) + pair(part).astype(F32)).astype(F32)
    g_mid = cots.astype(F32) + rms_back(unit_ffn, scale_ffn, gain_ffn, g_two)
    grad_gain_ffn = 0.5 * jnp.sum(g_two * unit_ffn, axis=0)
    g_branch = low(g_mid)
    g_gated = low(dot(g_branch, w_ssm, ((1,), (1,))))
    g_attn = low(dot(g_branch, w_att, ((1,), (1,))))
    grad_ssm = low(dot(gated, g_branch, ((0,), (0,))))
    grad_att = low(dot(attn, g_branch, ((0,), (0,))))
    g_proj, g_par = mixer_backward(proj, consts, attn, lse, y_own, states, g_gated, g_attn)
    grad_in = dot(normed, g_proj, ((0,), (0,)))
    part = low(dot(g_proj, w_in, ((1,), (1,)))).reshape(4, span, width)
    g_h1 = low(by_core(part).astype(F32) + swap_rows(part).astype(F32)).astype(F32)
    g_x = by_core(g_mid) + rms_back(by_core(unit_in), by_core(jnp.broadcast_to(scale_in, x.shape)), gain_in, g_h1)
    g_x = low(g_x)
    grad_gain_in = jnp.sum(g_h1 * by_core(unit_in), axis=(0, 1))
    head_grads = jnp.tile(jnp.pad(g_par[:3, :CHIP_HEADS].T, ((0, block - CHIP_HEADS), (0, 0))), (groups, 1))
    extra = jnp.concatenate([grad_gain_in[:, None], grad_gain_ffn[:, None], head_grads], axis=1)
    grad_in = low(lax.dynamic_update_slice(grad_in, extra, (0, T0 + CHIP_HEADS)))

    by_block = lambda v: v.reshape(groups, -1, v.shape[-1])
    if fast:
        parts = (by_block(grad_in), by_block(grad_gu), by_block(grad_dn))
        parts += tuple(by_block(v) for v in swap_columns(grad_ssm, grad_att))
        *reduced, output, returned = reduce_all(parts, out_rows, g_x)
        reduced = [v.astype(F32) for v in reduced]
    else:
        parts = [by_block(grad_in), by_block(grad_gu), by_block(grad_dn)]
        for v in (grad_ssm, grad_att):
            both = jnp.stack([v, plain_pair(v)])
            both = jnp.where(c == 0, both, both[::-1]).reshape(-1, width)
            parts.append(by_block(cut(both, width // 2 * c, width // 2)))
        reduced, output, returned = plain_reduce(parts, out_rows, g_x, y, c)
    r_in, r_gu, r_dn, r_ssm, r_att = reduced
    both = lambda start, size: [r_in[0, :, start : start + size], r_in[1, :, start : start + size]]
    grad_in_proj = jnp.concatenate(
        both(Z0, XW)
        + both(X0, XW)
        + [r_in[0, :, B0:T0] + r_in[1, :, B0:T0]]
        + both(Q0, QW)
        + both(KV0, HEAD_WIDTH)
        + both(KV0 + HEAD_WIDTH, HEAD_WIDTH),
        axis=1,
    )
    grad_dt_proj = jnp.concatenate(both(T0, CHIP_HEADS), axis=1)
    tail = r_in[:, :, T0 + CHIP_HEADS : T0 + CHIP_HEADS + 5]
    gains = tail[0, :, :2] + tail[1, :, :2]
    heads = tail[:, :CHIP_HEADS, 2:5].reshape(MH, 3)
    grad_gate_up = jnp.stack(
        [r_gu[k].reshape(block, 2, groups, half_units) for k in range(2)], axis=3
    ).reshape(block, 2 * FF)
    side = lambda v: jnp.concatenate([v[0], v[1]], axis=1)
    return (
        output,
        jnp.take(returned, jnp.argsort(deal_order), axis=0),
        gains[:, 0],
        grad_in_proj,
        grad_dt_proj,
        heads[:, 0],
        heads[:, 1],
        heads[:, 2],
        side(r_ssm),
        side(r_att),
        gains[:, 1],
        grad_gate_up,
        r_dn.reshape(-1, width),
    )


def solution(mesh):
    return jax.shard_map(
        body,
        mesh=mesh,
        in_specs=(
            P(None, "seq", "dp"),
            P("dp", "seq", None),
            P(),
            P(),
            P("dp"),
            P("dp", None),
            P("dp", None),
            P(),
            P(),
            P(),
            P("dp", None),
            P("dp", None),
            P("dp"),
            P("dp", None),
            P("dp", None),
        ),
        out_specs=(
            P("dp", "seq", None),
            P(None, "seq", "dp"),
            P("dp"),
            P("dp", None),
            P("dp", None),
            P(),
            P(),
            P(),
            P("dp", None),
            P("dp", None),
            P("dp"),
            P("dp", None),
            P("dp", None),
        ),
        check_vma=False,
    )
```

time: 1600 us -> 643 us (0.40)
  waiting for transfers between devices: 491 us -> 0 us
  Pallas kernels: 0 us -> 466 us
  matrix products: 357 us -> 78 us
  other arithmetic: 258 us -> 41.6 us
  local copies, waits for them, and re-layouts: 254 us -> 43.5 us
  blocking collectives: 136 us -> 0 us
  starting transfers between devices: 64.2 us -> 0 us
    pallas_call x0 -> x10, Pallas kernels: none -> 466 us  [the longest x1 187 us: reduce_all(): pl.pallas_call(reduce_kernel, name='reduce_and_return', out_shape=tuple(o...]
    reduce_scatter x6 -> x0, waiting for transfers between devices: 395 us -> none  [the longest x1 283 us: body(): lax.psum_scatter(matrices[0], 'dp', scatter_dimension=0, tiled=True)]
    dot_general x89 -> x15, matrix products: 357 us -> 78 us  [dot(): lax.dot_general(a, b, (dims, ((), ())), precision=precision, preferred_el...]
    another operation x49 -> x3, other arithmetic: 101 us -> 0.39 us
    all_gather x3 -> x0, blocking collectives: 89.4 us -> none  [the longest x1 54.8 us: body(): lax.all_gather(in_gain, 'dp', axis=0, tiled=True)]
    all_to_all x12 -> x0, starting transfers between devices: 63.1 us -> none  [the longest x1 12.9 us: body(): lax.all_to_all(dt_tok, 'seq', split_axis=2, concat_axis=1, tiled=True)]
    reshape x27 -> x3, local copies, waits for them, and re-layouts: 59.8 us -> 4.55 us  [the longest x1 2.68 us: body(): grad_gate_up = jnp.stack([r_gu[k].reshape(block, 2, groups, half_units) f...]
    convert_element_type x45 -> x12, other arithmetic: 64.3 us -> 17.3 us  [the longest x4 12.4 us: low(): return v.astype(BF)]
  transfers between devices with their start and end apart: 24 -> 0, of which waited for: 8 -> 0; matrix products, arithmetic and copies ran while one was open for 51% -> 0% of each run, Pallas kernels for 0% -> 0%
where the time goes in v1:
time: 643 us; the launch traced here: 633 us
  Pallas kernels  466 us (72%)
  matrix products  78 us (12%)
  local copies, waits for them, and re-layouts  43.5 us (7%)
  other arithmetic  41.6 us (6%)
    pallas_call x1, Pallas kernels, reduce_all(): pl.pallas_call(reduce_kernel, name='reduce_and_return', out_shape=tuple(o...  187 us
    pallas_call x1, Pallas kernels, gather_weights(): pl.pallas_call(gather_kernel, name='gather_weights', out_shape=(jax.Shape...  94.1 us
    dot_general x15, matrix products, dot(): lax.dot_general(a, b, (dims, ((), ())), precision=precision, preferred_el...  78 us
    pallas_call x1, Pallas kernels, start_transfers(): pl.pallas_call(start_kernel, name='deal_and_gather', out_shape=(jax.Shape...  72.4 us
    pallas_call x1, Pallas kernels, mixer_backward(): pl.pallas_call(backward_kernel, name='mixer_backward', out_shape=(jax.Sha...  35.6 us
    pallas_call x1, Pallas kernels, swap_columns(): pl.pallas_call(columns_kernel, name='swap_columns', out_shape=tuple((jax....  33.3 us
    pallas_call x4, Pallas kernels, pair_swap(): pl.pallas_call(functools.partial(pair_kernel, blocks), name='pair_swap_ro...  22.7 us
    pallas_call x1, Pallas kernels, mixer_forward(): pl.pallas_call(forward_kernel, name='mixer_forward', out_shape=(jax.Shape...  21 us

profile of v1, /device:TPU:9, one launch (start us, length us, event | category | flops | bytes accessed | tf_op | source)
XLA Modules:
  0.0 632.6 jit_solution(15539261494604164576)
XLA Ops:
  0.7 2.0 sort.17
  3.4 0.7 gather_fusion
  4.2 1.1 broadcast_select_fusion.1.dealt
  5.9 1.0 concatenate.29.w
  6.9 72.4 %deal_and_gather.1 = (bf16[4,256,1024]{2,1,0:T(8,128)(2,1)}, bf16[8,128,2304]{2,1,0:T(8,128)(2,1)}, bf16[4,256,1024]{2,1,0:T(8,128)(2,1)}) custom-call(bf16[16,256,128]{2,1,0:T(8,128)(2,1)} %broadcast_select_fusion.1.dealt, bf16[2,256,1024]{2,1,0:T(8,128)(2,1)} %cot.1, bf16[128,2304]{1,0:T(8,128)(2,1)} %concatenate.29.w), custom_call_target="tpu_custom_call" | custom-call | tf_op jit(solution)/shard_map/deal_and_gather/pallas_call | solution.py:492
  79.4 2.2 slice_convert_fusion
  82.8 1.3 copy-done.27
  84.1 6.7 %convolution_convert_fusion.proj = bf16[1024,2304]{1,0:T(8,128)(2,1)} fusion(bf16[1024,1024]{1,0:T(8,128)(2,1)S(1)} %bitcast.193, bf16[1024,2304]{1,0:T(8,128)(2,1)S(1)} %bitcast.208), kind=kOutput, calls=%fused_computation.2 | convolution fusion | flops 4834197504 | bytes 11534336 | tf_op jit(solution)/shard_map/dot_general | solution.py:36
  91.4 1.0 copy.98.cosine
  92.5 1.0 copy.99.sine
  96.5 1.0 broadcast_in_dim.30.segc
  98.4 0.8 compare_convert_fusion.spread
  100.0 21.0 %mixer_forward.1 = (bf16[1024,768]{1,0:T(8,128)(2,1)}, bf16[1024,256]{1,0:T(8,128)(2,1)}, f32[1024,128]{1,0:T(8,128)}, f32[1024,768]{1,0:T(8,128)}, f32[4,128,768]{2,1,0:T(8,128)}) custom-call(bf16[1024,2304]{1,0:T(8,128)(2,1)} %convolution_convert_fusion.proj, f32[1024,128]{1,0:T(8,128)} %copy.98.cosine, f32[1024,128]{1,0:T(8,128)} %copy.99.sine, ...), custom_call_target="tpu_custom_call" | custom-call | tf_op jit(solution)/shard_map/mixer_forward/pallas_call | solution.py:309
  121.1 0.7 constant_dynamic-slice_fusion.4.ssm
  122.4 1.8 reshape.350
  124.2 3.1 dynamic-slice_reduce_fusion
  127.3 0.9 copy.140
  128.2 1.7 constant_dynamic-slice_fusion.2.dn
  129.9 94.1 %gather_weights.1 = (bf16[4,192,1024]{2,1,0:T(8,128)(2,1)}, bf16[4,64,1024]{2,1,0:T(8,128)(2,1)}, bf16[8,128,2048]{2,1,0:T(8,128)(2,1)}, bf16[8,128,1024]{2,1,0:...) custom-call(bf16[192,512]{1,0:T(8,128)(2,1)} %constant_dynamic-slice_fusion.4.ssm, ...), custom_call_target="tpu_custom_call" | custom-call | tf_op jit(solution)/shard_map/gather_weights/pallas_call | solution.py:548
  224.0 3.8 fusion.41
  227.8 2.1 add_convert_fusion.1.part
  229.9 12.1 %pair_swap.2 = bf16[1024,1024]{1,0:T(8,128)(2,1)} custom-call(bf16[1024,1024]{1,0:T(8,128)(2,1)} %add_convert_fusion.1.part), custom_call_target="tpu_custom_call" | custom-call | tf_op jit(solution)/shard_map/pair_swap/pallas_call | solution.py:588
  242.0 6.5 %multiply_reduce_fusion = (f32[1024]{0:T(1024)S(1)}, f32[1024,1024]{1,0:T(8,128)}, bf16[1024,1024]{1,0:T(8,128)(2,1)}) fusion(bf16[1024,1024]{1,0:T(8,128)(2,1)} %pair_swap.2, bf16[1024,1024]{1,0:T(8,128)(2,1)} %add_convert_fusion.1.part, bf16[4,256,1024]{2,1,0:T(8,128)(2,1)S(1)} %copy-done.3, f32[1024]{0:T(1024)S(1)} %bitcast.203, f32[1024]{0:T(1024)S(1)} %bitcast.214), kind=kLoop, calls=%fused_computation.32 | loop fusion | flops 10484736 | bytes 12595200 | tf_op jit(solution)/shard_map/reduce_sum | solution.py:814
  248.6 8.2 %convert_convert_fusion = f32[1024,2048]{0,1:T(8,128)S(1)} fusion(bf16[1024,2048]{1,0:T(8,128)(2,1)} %bitcast.220, f32[1024,1024]{1,0:T(8,128)} %get-tuple-element.122, f32[1024]{0:T(1024)S(1)} %bitcast.209, f32[1024]{0:T(1024)S(1)} %add_rsqrt_fusion), kind=kOutput, calls=%fused_computation.30 | convolution fusion | flops 4302307328 | bytes 16785408 | tf_op jit(solution)/shard_map/dot_general | solution.py:36
  256.9 5.1 fusion.6
  262.0 1.3 copy-done.44
  263.9 5.8 fusion.26.part
  269.7 4.5 pair_swap.3
  274.3 5.0 fusion.8
  280.2 4.8 fusion.38
  285.0 3.0 convolution_convert_fusion.7.ggated
  288.0 1.5 convolution_convert_fusion.9.gattn
  289.5 35.6 %mixer_backward.1 = (bf16[1024,2304]{1,0:T(8,128)(2,1)}, f32[8,128]{1,0:T(8,128)}) custom-call(bf16[1024,2304]{1,0:T(8,128)(2,1)} %convolution_convert_fusion.proj, f32[1024,128]{1,0:T(8,128)} %copy.98.cosine, f32[1024,128]{1,0:T(8,128)} %copy.99.sine, s32[1024,128]{1,0:T(8,128)} %broadcast_in_dim.30.segc, s32[8,1024]{1,0:T(8,128)} %broadcast_in_dim.31.segr, ...), custom_call_target="tpu_custom_call" | custom-call | tf_op jit(solution)/shard_map/mixer_backward/pallas_call | solution.py:328
  325.1 9.2 %fusion.42 = bf16[1024,2304]{1,0:T(8,128)(2,1)} fusion(bf16[1024,1024]{1,0:T(8,128)(2,1)S(1)} %copy-done.18, bf16[1024,2304]{1,0:T(8,128)(2,1)} %get-tuple-element.74), kind=kOutput, calls=%fused_computation.153 | convolution fusion | flops 4831838208 | bytes 11534336 | tf_op jit(solution)/shard_map/dot_general | solution.py:36
  335.1 9.3 %convolution_convert_fusion.4 = bf16[1024,1024]{1,0:T(8,128)(2,1)} fusion(bf16[1024,2304]{1,0:T(8,128)(2,1)} %get-tuple-element.74, bf16[1024,2304]{1,0:T(8,128)(2,1)} %bitcast.207), kind=kOutput, calls=%fused_computation.56 | convolution fusion | flops 4832886784 | bytes 11534336 | tf_op jit(solution)/shard_map/dot_general | solution.py:36
  344.4 3.0 pair_swap_rows.2
  347.9 1.1 copy-done.12
  349.3 1.7 fusion.18
  351.1 0.7 copy-done.6
  352.0 3.4 dynamic_update_slice.3
  355.5 9.9 %convolution_convert_fusion.1 = bf16[1024,2048]{1,0:T(8,128)(2,1)} fusion(bf16[1024,1024]{0,1:T(8,128)(2,1)} %copy-done.46, bf16[1024,1024]{0,1:T(8,128)(2,1)S(1)} %copy-done.45, f32[1024,1024]{1,0:T(8,128)} %get-tuple-element.122, f32[1024]{0:T(1024)S(1)} %bitcast.212, f32[1024]{0:T(1024)S(1)} %add_rsqrt_fusion), kind=kOutput, calls=%fused_computation.34 | convolution fusion | flops 4308598784 | bytes 12591104 | tf_op jit(solution)/shard_map/dot_general | solution.py:36
  365.4 3.7 convolution_convert_fusion.3
  369.1 3.0 convolution_convert_fusion.6
  372.1 1.5 convolution_convert_fusion.8
  373.6 33.3 %swap_columns.1 = (bf16[8,192,512]{2,1,0:T(8,128)(2,1)}, bf16[8,64,512]{2,1,0:T(8,128)(2,1)}) custom-call(bf16[4,192,1024]{2,1,0:T(8,128)(2,1)} %bitcast.199, bf16[4,64,1024]{2,1,0:T(8,128)(2,1)} %bitcast.197), custom_call_target="tpu_custom_call" | custom-call | tf_op jit(solution)/shard_map/swap_columns/pallas_call | solution.py:618
  406.9 5.3 convolution_convert_fusion.2
  412.3 3.0 pair_swap_rows.3
  415.3 3.6 fusion.24.refs_5_
  418.9 3.4 fusion.21.refs_6_
  422.3 186.6 %reduce_and_return.1 = (bf16[2,128,2304]{2,1,0:T(8,128)(2,1)}, bf16[2,128,2048]{2,1,0:T(8,128)(2,1)}, bf16[2,128,1024]{2,1,0:T(8,128)(2,1)}, bf16[2,192,512]{2,1...) custom-call(bf16[8,128,2304]{2,1,0:T(8,128)(2,1)} %bitcast.186, ...), custom_call_target="tpu_custom_call" | custom-call | tf_op jit(solution)/shard_map/reduce_and_return/pallas_call | solution.py:764
  608.9 2.0 gather_fusion.1
  610.9 1.1 broadcast_select_fusion
  612.8 0.7 slice_reduce_fusion
  613.5 1.0 slice_bitcast_fusion.4
  614.6 0.8 slice_bitcast_fusion.14
  615.4 3.2 concatenate.33
  619.3 0.8 slice.205
  620.8 1.1 convert_element_type.245
  622.0 0.9 pad_maximum_fusion.6
  623.0 0.7 pad_maximum_fusion.8
  624.7 1.6 copy.111
  626.3 2.7 reshape.366
  629.0 2.2 bitcast_convert_fusion
  631.2 1.0 copy.145
  (164 shorter events, 13.4 us)
Async XLA Ops:
  0.6 2.7 copy-start
  0.7 3.5 copy-start.32
  3.3 2.0 copy-start.24
  4.1 1.4 copy-start.30
  4.1 1.5 copy-start.33
  4.1 1.7 copy-start.34
  79.4 2.4 copy-start.3
  81.7 2.4 copy-start.27
  91.3 4.7 copy-start.31
  91.4 6.7 %copy-start.35 = (f32[24]{0:T(128)S(1)}, f32[24]{0:T(128)}, u32[]{:S(2)}) copy-start(f32[24]{0:T(128)} %param.29) | copy-start | bytes 292
  91.4 6.7 %copy-start.36 = (f32[24]{0:T(128)S(1)}, f32[24]{0:T(128)}, u32[]{:S(2)}) copy-start(f32[24]{0:T(128)} %param.28) | copy-start | bytes 292
  91.4 7.8 %copy-start.42 = (f32[24]{0:T(128)S(1)}, f32[24]{0:T(128)}, u32[]{:S(2)}) copy-start(f32[24]{0:T(128)} %param.30) | copy-start | bytes 292
  98.4 1.6 copy-start.28
  100.0 21.0 %copy-start.26 = (bf16[192,1024]{1,0:T(8,128)(2,1)S(1)}, bf16[192,1024]{1,0:T(8,128)(2,1)}, u32[]{:S(2)}) copy-start(bf16[192,1024]{1,0:T(8,128)(2,1)} %param.31) | copy-start | bytes 1179652
  100.0 21.7 %copy-start.29 = (bf16[64,1024]{1,0:T(8,128)(2,1)S(1)}, bf16[64,1024]{1,0:T(8,128)(2,1)}, u32[]{:S(2)}) copy-start(bf16[64,1024]{1,0:T(8,128)(2,1)} %param.32) | copy-start | bytes 393220
  224.0 3.8 copy-start.10
  224.0 3.8 copy-start.23
  242.0 6.5 %copy-start.19 = (f32[1024,1]{1,0:T(8,128)S(1)}, f32[1024,1]{1,0:T(8,128)}, u32[]{:S(2)}) copy-start(f32[1024,1]{1,0:T(8,128)} %get-tuple-element.126) | copy-start | bytes 12292
  248.6 8.2 %copy-start.16 = (bf16[4,256,1024]{2,1,0:T(8,128)(2,1)S(1)}, bf16[4,256,1024]{2,1,0:T(8,128)(2,1)}, u32[]{:S(2)}) copy-start(bf16[4,256,1024]{2,1,0:T(8,128)(2,1)} %get-tuple-element.68) | copy-start | bytes 6291460
  248.6 8.2 %copy-start.38 = (bf16[8,128,1024]{2,1,0:T(8,128)(2,1)S(1)}, bf16[8,128,1024]{2,1,0:T(8,128)(2,1)}, u32[]{:S(2)}) copy-start(bf16[8,128,1024]{2,1,0:T(8,128)(2,1)} %get-tuple-element.72) | copy-start | bytes 6291460
  256.9 7.0 %copy-start.37 = (bf16[8,128,2048]{2,1,0:T(8,128)(2,1)S(1)}, bf16[8,128,2048]{2,1,0:T(8,128)(2,1)}, u32[]{:S(2)}) copy-start(bf16[8,128,2048]{2,1,0:T(8,128)(2,1)} %get-tuple-element.73) | copy-start | bytes 12582916
  262.0 1.3 copy-start.44
  262.0 2.0 copy-start.46
  274.3 5.0 copy-start.2
  274.3 5.3 copy-start.4
  274.3 5.9 copy-start.5
  280.2 4.8 copy-start.41
  285.0 3.0 copy-start.8
  289.5 35.6 %copy-start.18 = (bf16[1024,1024]{1,0:T(8,128)(2,1)S(1)}, bf16[1024,1024]{1,0:T(8,128)(2,1)}, u32[]{:S(2)}) copy-start(bf16[1024,1024]{1,0:T(8,128)(2,1)} %get-tuple-element.143) | copy-start | bytes 6291460
  347.5 1.6 copy-start.12
  347.5 1.8 copy-start.15
  349.3 2.5 copy-start.6
  349.3 6.1 copy-start.45
  355.5 9.9 %copy-start.17 = (bf16[4,256,1024]{2,1,0:T(8,128)(2,1)S(1)}, bf16[4,256,1024]{2,1,0:T(8,128)(2,1)}, u32[]{:S(2)}) copy-start(bf16[4,256,1024]{2,1,0:T(8,128)(2,1)} %get-tuple-element.68) | copy-start | bytes 6291460
  355.5 9.9 %copy-start.43 = (bf16[1024,1024]{0,1:T(8,128)(2,1)S(1)}, bf16[1024,1024]{0,1:T(8,128)(2,1)}, u32[]{:S(2)}) copy-start(bf16[1024,1024]{0,1:T(8,128)(2,1)} %get-tuple-element.125) | copy-start | bytes 6291460
  365.4 3.7 copy-start.9
  365.4 3.7 copy-start.40
  369.1 3.0 copy-start.11
  372.1 34.8 %copy-start.39 = (bf16[8,128,1024]{2,1,0:T(8,128)(2,1)S(1)}, bf16[8,128,1024]{2,1,0:T(8,128)(2,1)}, u32[]{:S(2)}) copy-start(bf16[8,128,1024]{2,1,0:T(8,128)(2,1)} %get-tuple-element.72) | copy-start | bytes 6291460
  412.3 3.0 copy-start.13
  415.3 3.6 copy-start.7
  415.3 3.6 copy-start.14
  610.9 1.6 copy-start.20
  620.8 2.1 copy-start.25
  621.9 1.8 copy-start.21
  626.3 5.9 copy-start.1
  629.0 2.2 copy-start.22

commit v2 on v1

--- a/solution.py
+++ b/solution.py
@@ -77,7 +77,7 @@
     return kk.astype(BF), vv.astype(BF)
 
 
-def attention_forward(proj_ref, cos_ref, sin_ref, segc_ref, segr_ref, attn_ref, lse_ref):
+def attention_forward(proj_ref, cos_ref, sin_ref, segc_ref, segr_ref, attn_ref, lse_ref, tick):
     seq_len = proj_ref.shape[0]
     kk, vv = key_value_pairs(proj_ref[:, KV0 : KV0 + 128].astype(F32), cos_ref[...], sin_ref[...])
     low = lanes(QB) < 64
@@ -98,11 +98,12 @@
                 total = jnp.sum(e, axis=1, keepdims=True)
                 outs.append(dot(e.astype(BF), vv[:upto]) / total)
                 tops = jnp.where(lanes(QB) == 2 * pair + half, top + jnp.log(total), tops)
+                tick()
             attn_ref[rows, 128 * pair : 128 * (pair + 1)] = jnp.where(low, outs[0], outs[1]).astype(BF)
         lse_ref[rows, :] = tops
 
 
-def attention_backward(proj_ref, cos_ref, sin_ref, segc_ref, segr_ref, attn_ref, lse_ref, gattn_ref, gproj_ref, gkv):
+def attention_backward(proj_ref, cos_ref, sin_ref, segc_ref, segr_ref, attn_ref, lse_ref, gattn_ref, gproj_ref, gkv, tick):
     seq_len = proj_ref.shape[0]
     kk, vv = key_value_pairs(proj_ref[:, KV0 : KV0 + 128].astype(F32), cos_ref[...], sin_ref[...])
     low = lanes(QB) < 64
@@ -136,6 +137,7 @@
                 gkv[0:upto, 0:128] += dot(gs, qh)
                 gkv[0:upto, 128:256] += dot(p.astype(BF), gh)
                 grads.append(dot(gs, kk[:upto], ((0,), (0,))))
+                tick()
             gq = jnp.where(low, grads[0], grads[1]) * HEAD_WIDTH**-0.5
             gproj_ref[rows, Q0 + 128 * pair : Q0 + 128 * (pair + 1)] = turn_back(gq, cosine, sine).astype(BF)
     gk = gkv[:, 0:128]
@@ -146,10 +148,9 @@
 
 
 def scan_pieces(j, proj_ref, segc_ref, segr_ref, par_ref):
-    rows = pl.ds(pl.multiple_of(j * CHUNK, CHUNK), CHUNK)
+    rows = pl.ds(j * CHUNK, CHUNK)
     seg = segc_ref[rows, :]
-    prev = segc_ref[pl.ds(jnp.maximum(j * CHUNK - 1, 0), 1), :]
-    prev = jnp.where(j == 0, -1, prev)
+    prev = segc_ref[pl.ds(j * CHUNK - 1, 1), :] if j else jnp.full((1, 128), -1, jnp.int32)
     last = segc_ref[pl.ds(j * CHUNK + CHUNK - 1, 1), :]
     valid = lanes(CHUNK) < CHIP_HEADS
     raw = proj_ref[rows, T0 : T0 + 128].astype(F32) + par_ref[0:1, :]
@@ -165,11 +166,11 @@
     return rows, raw, dt, decay, cum, from_start, to_end, keep, under
 
 
-def scan_forward(proj_ref, segc_ref, segr_ref, par_ref, spread_ref, wide_ref, gated_ref, y_ref, states_ref, state):
+def scan_forward(proj_ref, segc_ref, segr_ref, par_ref, spread_ref, wide_ref, gated_ref, y_ref, states_ref, state, tick):
     spread = spread_ref[...]
     state[...] = jnp.zeros_like(state)
 
-    def chunk(j, carry):
+    for j in range(proj_ref.shape[0] // CHUNK):
         rows, raw, dt, decay, cum, from_start, to_end, keep, under = scan_pieces(j, proj_ref, segc_ref, segr_ref, par_ref)
         place = lax.broadcasted_iota(jnp.int32, (CHUNK, CHUNK), 0)
         same = segc_ref[rows, 0:1] == segr_ref[0:1, rows]
@@ -199,15 +200,13 @@
             y = (local + x[:, cols] * wide_ref[0:1, cols]).astype(BF).astype(F32)
             z = proj_ref[rows, Z0 + 128 * pair : Z0 + 128 * (pair + 1)].astype(F32)
             gated_ref[rows, cols] = (y * (z / (1.0 + jnp.exp(-z)))).astype(BF)
+            tick()
         weighted = (xdt * widen(to_end, spread)).astype(BF)
         keep_wide = widen(jnp.broadcast_to(keep, (8, 128)), spread)[0:1, :]
         state[...] = old * keep_wide + dot(b, weighted, ((0,), (0,)))
-        return carry
-
-    lax.fori_loop(0, proj_ref.shape[0] // CHUNK, chunk, 0)
-
-
-def scan_backward(proj_ref, segc_ref, segr_ref, par_ref, spread_ref, wide_ref, y_ref, states_ref, ggated_ref, gproj_ref, gpar_ref, gstate):
+
+
+def scan_backward(proj_ref, segc_ref, segr_ref, par_ref, spread_ref, wide_ref, y_ref, states_ref, ggated_ref, gproj_ref, gpar_ref, gstate, tick):
     spread = spread_ref[...]
     gstate[...] = jnp.zeros_like(gstate)
     gpar_ref[...] = jnp.zeros_like(gpar_ref)
@@ -218,8 +217,7 @@
         rest = (v - top.astype(F32)).astype(BF)
         return dot(top, spread, ((1,), (1,))) + dot(rest, spread, ((1,), (1,)))
 
-    def chunk(step, carry):
-        j = chunks - 1 - step
+    for j in reversed(range(chunks)):
         rows, raw, dt, decay, cum, from_start, to_end, keep, under = scan_pieces(j, proj_ref, segc_ref, segr_ref, par_ref)
         place = lax.broadcasted_iota(jnp.int32, (CHUNK, CHUNK), 0)
         same = segc_ref[rows, 0:1] == segr_ref[0:1, rows]
@@ -260,6 +258,7 @@
                 total = total + dot(mix, gh)
                 gbc = gbc + dot(xp, gh, ((1,), (1,))) * spread_h
             gxdt.append(total)
+            tick()
         gxdt = jnp.concatenate(gxdt, axis=1)
         gstart = (gy * start_wide).astype(BF)
         weighted = (xdt_low.astype(F32) * end_wide).astype(BF)
@@ -284,59 +283,26 @@
         gpar_ref[1:2, :] += jnp.sum(gdecay * decay, axis=0, keepdims=True)
         skip = jnp.sum(gy * x, axis=0, keepdims=True)
         gpar_ref[2:3, :] += narrow(jnp.broadcast_to(skip, (8, XW)))[0:1, :]
-        return carry
-
-    lax.fori_loop(0, chunks, chunk, 0)
-
-
-def forward_kernel(proj, cosine, sine, segc, segr, par, spread, wide, gated, attn, lse, y, states, state):
-    attention_forward(proj, cosine, sine, segc, segr, attn, lse)
-    scan_forward(proj, segc, segr, par, spread, wide, gated, y, states, state)
-
-
-def backward_kernel(proj, cosine, sine, segc, segr, par, spread, wide, attn, lse, y, states, ggated, gattn, gproj, gpar, gkv, gstate):
-    attention_backward(proj, cosine, sine, segc, segr, attn, lse, gattn, gproj, gkv)
-    scan_backward(proj, segc, segr, par, spread, wide, y, states, ggated, gproj, gpar, gstate)
+
+
+class Ticker:
+    def __init__(self, steps, ticks):
+        self.steps, self.ticks, self.calls, self.done = steps, ticks, 0, 0
+
+    def __call__(self):
+        self.calls += 1
+        while self.done < len(self.steps) and self.done * self.ticks < self.calls * len(self.steps):
+            self.steps[self.done]()
+            self.done += 1
+
+    def drain(self):
+        while self.done < len(self.steps):
+            self.steps[self.done]()
+            self.done += 1
 
 
 def whole(n):
     return [pl.BlockSpec(memory_space=VM)] * n
-
-
-def mixer_forward(proj, consts):
-    seq_len = proj.shape[0]
-    chunks = seq_len // CHUNK
-    return pl.pallas_call(
-        forward_kernel,
-        name="mixer_forward",
-        out_shape=(
-            jax.ShapeDtypeStruct((seq_len, XW), BF),
-            jax.ShapeDtypeStruct((seq_len, QW), BF),
-            jax.ShapeDtypeStruct((seq_len, 128), F32),
-            jax.ShapeDtypeStruct((seq_len, XW), F32),
-            jax.ShapeDtypeStruct((chunks, NS, XW), F32),
-        ),
-        in_specs=whole(8),
-        out_specs=tuple(whole(5)),
-        scratch_shapes=[VM((NS, XW), F32)],
-        compiler_params=pltpu.CompilerParams(vmem_limit_bytes=56 * MIB),
-    )(proj, *consts)
-
-
-def mixer_backward(proj, consts, attn, lse, y, states, ggated, gattn):
-    seq_len = proj.shape[0]
-    return pl.pallas_call(
-        backward_kernel,
-        name="mixer_backward",
-        out_shape=(
-            jax.ShapeDtypeStruct((seq_len, COLS), BF),
-            jax.ShapeDtypeStruct((8, 128), F32),
-        ),
-        in_specs=whole(14),
-        out_specs=tuple(whole(2)),
-        scratch_shapes=[VM((seq_len, 256), F32), VM((NS, XW), F32)],
-        compiler_params=pltpu.CompilerParams(vmem_limit_bytes=56 * MIB),
-    )(proj, *consts, attn, lse, y, states, ggated, gattn)
 
 
 def place():
@@ -370,6 +336,7 @@
 
 
 ARRAY_SENDS = 13
+CORNER_X = 3
 
 
 class Gather:
@@ -399,14 +366,19 @@
             self.push(r - 1, self.src.at[self.mine], target, self.dst.at[own, self.mine])
         self.push(3, self.src, self.xpeer, self.dst.at[own])
 
+    def cross(self):
+        landed(self.block(0, 1 - self.x, slice(None)), self.sems, self.base + 3, self.xpeer)
+        self.push(4, self.block(0, 1 - self.x, self.mine), device(self.z ^ 1, self.x, self.y, self.c))
+
     def forward(self, r):
         ref = self.block(r, self.x, self.mine)
         landed(ref, self.sems, self.base + r - 1, self.xpeer)
-        self.push(3 + r, ref, self.xpeer)
         self.push(6 + r, ref, self.ypeer)
+        if r > 1:
+            self.push(3 + r, ref, self.xpeer)
 
     def corner(self, r):
-        if r == 1:
+        if r == CORNER_X:
             ref = self.block(r, self.x, self.other)
             landed(ref, self.sems, self.base + 6 + r, self.ypeer)
             self.push(9 + r, ref, self.xpeer)
@@ -415,17 +387,70 @@
             landed(ref, self.sems, self.base + 3 + r, self.xpeer)
             self.push(9 + r, ref, self.ypeer)
 
-    def finish(self):
-        landed(self.dst.at[2 * self.z + 1 - self.x], self.sems, self.base + 3, self.xpeer)
+    def arrive(self):
         for r in (1, 2, 3):
-            if r == 1:
+            if r == CORNER_X:
                 landed(self.block(r, 1 - self.x, self.mine), self.sems, self.base + 3 + r, self.xpeer)
             else:
                 landed(self.block(r, self.x, self.other), self.sems, self.base + 6 + r, self.ypeer)
             landed(self.block(r, 1 - self.x, self.other), self.sems, self.base + 9 + r, self.ypeer)
+        self.local.wait()
+
+    def finish(self):
         for copy in self.sent:
             copy.wait_send()
-        self.local.wait()
+
+
+def gather_steps(gathers):
+    def one(g):
+        return [
+            lambda: g.forward(1),
+            g.cross,
+            lambda: g.forward(2),
+            lambda: g.forward(3),
+        ]
+
+    def corners(g):
+        return [lambda r=r: g.corner(r) for r in (2, 3, 1)]
+
+    steps = []
+    count = len(gathers)
+    for k in range(count + 1):
+        if k + 1 < count:
+            steps.append(gathers[k + 1].start)
+        ahead = one(gathers[k]) if k < count else []
+        behind = corners(gathers[k - 1]) if k else []
+        steps += ahead[:2] + behind[:1] + ahead[2:3] + behind[1:2] + ahead[3:] + behind[2:]
+    return steps
+
+
+def reduce_steps(sums, partner):
+    def early(s):
+        return [
+            lambda: s.relay(1),
+            lambda: s.relay(2),
+            lambda: s.root(1),
+            lambda: s.relay(3),
+            s.cross,
+            lambda: s.relay(0),
+        ]
+
+    def late(s):
+        return [lambda r=r: s.root(r) for r in (2, 3, 0)]
+
+    steps = []
+    for k in range(len(sums) + 3):
+        if k < len(sums):
+            if k + 1 < len(sums):
+                steps.append(sums[k + 1].start)
+            steps += early(sums[k])
+        if 0 <= k - 1 < len(sums):
+            steps += late(sums[k - 1])
+        if 0 <= k - 2 < len(sums):
+            steps.append(lambda s=sums[k - 2]: s.total(partner))
+        if 0 <= k - 3 < len(sums):
+            steps.append(lambda s=sums[k - 3]: s.spread(partner))
+    return steps
 
 
 def chip_peers():
@@ -435,12 +460,11 @@
     return peers
 
 
-def start_kernel(dealt, cot, w, rows, weights, gcot, dsend, drecv, wsend, wrecv, local):
+def start_kernel(dealt, w, rows, weights, dsend, drecv, wsend, wrecv, local):
     z, x, y, c = place()
     own = 2 * z + x
     slot = 2 * y + c
     partner = device(z, x, y, 1 - c)
-    ypeer = device(z, x, 1 - y, c)
     others = [(r, i, j) for r in range(4) for i in range(2) for j in range(2) if r or i or j]
     targets = [device(z ^ r, x ^ i, y ^ j, c) for r, i, j in others]
     greet(targets + [partner])
@@ -448,18 +472,16 @@
     gather = Gather(w, weights, (wsend, wrecv), 0, local.at[0])
     columns = lambda d: pl.ds(pl.multiple_of(d * 128, 128), 128)
     sent = []
+    gather.start()
     for k, (r, i, j) in enumerate(others):
         pack = 2 * (2 * (z ^ r) + (x ^ i)) + (y ^ j)
         sent.append(send(dealt.at[pack], rows.at[slot, :, columns(own)], sems, k, targets[k]))
     here = pltpu.make_async_copy(dealt.at[2 * own + y], rows.at[slot, :, columns(own)], local.at[1])
     here.start()
-    gather.start()
-    sent.append(send(cot.at[1 - y], gcot.at[slot], sems, 18, ypeer))
-    sent.append(send(cot.at[y], gcot.at[slot], sems, 19, partner))
-    mine = pltpu.make_async_copy(cot.at[y], gcot.at[slot], local.at[2])
-    mine.start()
-    for r in (1, 2, 3):
-        gather.forward(r)
+    gather.forward(1)
+    gather.cross()
+    gather.forward(2)
+    gather.forward(3)
     here.wait()
     for same_y in (True, False):
         for k, (r, i, j) in enumerate(others):
@@ -470,24 +492,19 @@
         sent.append(send(ref, ref, sems, 15 if same_y else 16, partner))
     for r in (1, 2, 3):
         gather.corner(r)
-    ref = gcot.at[2 * (1 - y) + c]
-    landed(ref, sems, 18, ypeer)
-    sent.append(send(ref, ref, sems, 17, partner))
     landed(rows.at[2 * y + 1 - c], sems, 15, partner)
     landed(rows.at[2 * (1 - y) + 1 - c], sems, 16, partner)
-    landed(gcot.at[2 * (1 - y) + 1 - c], sems, 17, partner)
-    landed(gcot.at[2 * y + 1 - c], sems, 19, partner)
+    gather.arrive()
     for copy in sent:
         copy.wait_send()
     gather.finish()
-    mine.wait()
 
 
 def any_specs(n):
     return [pl.BlockSpec(memory_space=pl.ANY)] * n
 
 
-def start_transfers(dealt, cot, w):
+def start_transfers(dealt, w):
     packs, span, width = dealt.shape
     return pl.pallas_call(
         start_kernel,
@@ -495,79 +512,164 @@
         out_shape=(
             jax.ShapeDtypeStruct((4, span, 8 * width), BF),
             jax.ShapeDtypeStruct((8,) + w.shape, BF),
-            jax.ShapeDtypeStruct((4,) + cot.shape[1:], BF),
         ),
-        in_specs=any_specs(3),
-        out_specs=tuple(any_specs(3)),
+        in_specs=whole(2),
+        out_specs=tuple(any_specs(2)),
         scratch_shapes=[
-            pltpu.SemaphoreType.DMA((20,)),
-            pltpu.SemaphoreType.DMA((20,)),
+            pltpu.SemaphoreType.DMA((17,)),
+            pltpu.SemaphoreType.DMA((17,)),
             pltpu.SemaphoreType.DMA((ARRAY_SENDS,)),
             pltpu.SemaphoreType.DMA((ARRAY_SENDS,)),
-            pltpu.SemaphoreType.DMA((3,)),
+            pltpu.SemaphoreType.DMA((2,)),
         ],
         compiler_params=pltpu.CompilerParams(collective_id=0, has_side_effects=True),
-    )(dealt, cot, w)
-
-
-def gather_kernel(ssm, att, gu, dn, ssm_own, att_own, gu_all, dn_all, ssm_all, att_all, gsend, grecv, csend, crecv, local):
-    z, x, y, c = place()
-    partner = device(z, x, y, 1 - c)
+    )(dealt, w)
+
+
+class Cotangents:
+    def __init__(self, src, dst, sems, local_sem):
+        self.src, self.dst, self.sems, self.local_sem = src, dst, sems, local_sem
+        self.z, self.x, self.y, self.c = place()
+        self.slot = 2 * self.y + self.c
+        self.partner = device(self.z, self.x, self.y, 1 - self.c)
+        self.ypeer = device(self.z, self.x, 1 - self.y, self.c)
+
+    def start(self):
+        src, dst = self.src, self.dst
+        self.sent = [
+            send(src.at[1 - self.y], dst.at[self.slot], self.sems, 0, self.ypeer),
+            send(src.at[self.y], dst.at[self.slot], self.sems, 1, self.partner),
+        ]
+        self.local = pltpu.make_async_copy(src.at[self.y], dst.at[self.slot], self.local_sem)
+        self.local.start()
+
+    def forward(self):
+        ref = self.dst.at[2 * (1 - self.y) + self.c]
+        landed(ref, self.sems, 0, self.ypeer)
+        self.sent.append(send(ref, ref, self.sems, 2, self.partner))
+
+    def arrive(self):
+        landed(self.dst.at[2 * self.y + 1 - self.c], self.sems, 1, self.partner)
+        landed(self.dst.at[2 * (1 - self.y) + 1 - self.c], self.sems, 2, self.partner)
+        self.local.wait()
+
+    def finish(self):
+        for copy in self.sent:
+            copy.wait_send()
+
+
+class Halves:
+    def __init__(self, gather, dst, sems, base, local_sem):
+        self.gather, self.dst, self.sems, self.base, self.local_sem = gather, dst, sems, base, local_sem
+        z, x, y, self.c = place()
+        self.partner = device(z, x, y, 1 - self.c)
+
+    def columns(self, k):
+        half = self.gather.src.shape[1]
+        return self.dst.at[:, :, pl.ds(pl.multiple_of(k * half, 128), half)]
+
+    def start(self):
+        src, c = self.gather.dst, self.c
+        self.gather.arrive()
+        self.local = pltpu.make_async_copy(src.at[pl.ds(4 * c, 4)], self.columns(c), self.local_sem)
+        self.local.start()
+        self.sent = send(src.at[pl.ds(4 * (1 - c), 4)], self.columns(c), self.sems, self.base, self.partner)
+
+    def arrive(self):
+        landed(self.columns(1 - self.c), self.sems, self.base, self.partner)
+        self.local.wait()
+        self.sent.wait_send()
+
+
+def forward_kernel(*refs):
+    proj, cosine, sine, segc, segr, par, spread, wide, cot, *refs = refs
+    ssm, att, gu, dn, *refs = refs
+    gated, attn, lse, y_own, states, gcot, ssm_own, att_own, gu_all, dn_all, *refs = refs
+    state, ssm_all, att_all, gsend, grecv, csend, crecv, local = refs
     greet(chip_peers())
     sems = (gsend, grecv)
     pairs = ((ssm, ssm_all), (att, att_all), (gu, gu_all), (dn, dn_all))
     gathers = [Gather(a, b, sems, ARRAY_SENDS * i, local.at[i]) for i, (a, b) in enumerate(pairs)]
+    cots = Cotangents(cot, gcot, (csend, crecv), local.at[6])
+    halves = [Halves(g, out, (csend, crecv), 3 + i, local.at[4 + i]) for i, (g, out) in enumerate(zip(gathers, (ssm_own, att_own)))]
+    gathers[0].start()
+    cots.start()
+    ticker = Ticker(gather_steps(gathers) + [cots.forward], 40)
+    attention_forward(proj, cosine, sine, segc, segr, attn, lse, ticker)
+    scan_forward(proj, segc, segr, par, spread, wide, gated, y_own, states, state, ticker)
+    ticker.drain()
+    for h in halves:
+        h.start()
+    for g in gathers[2:]:
+        g.arrive()
+    cots.arrive()
+    for h in halves:
+        h.arrive()
     for g in gathers:
-        g.start()
-    for g in gathers:
-        for r in (1, 2, 3):
-            g.forward(r)
-    for g in gathers:
-        for r in (1, 2, 3):
-            g.corner(r)
-    sent = []
-    for i, (g, out) in enumerate(zip(gathers[:2], (ssm_own, att_own))):
         g.finish()
-        half = g.src.shape[1]
-        columns = lambda k: pl.ds(pl.multiple_of(k * half, 128), half)
-        here = pltpu.make_async_copy(g.dst.at[pl.ds(4 * c, 4)], out.at[:, :, columns(c)], local.at[4 + i])
-        here.start()
-        sent.append(here)
-        sent.append(send(g.dst.at[pl.ds(4 * (1 - c), 4)], out.at[:, :, columns(c)], (csend, crecv), i, partner))
-    for g in gathers[2:]:
-        g.finish()
-    for i, out in enumerate((ssm_own, att_own)):
-        half = out.shape[2] // 2
-        landed(out.at[:, :, pl.ds(pl.multiple_of((1 - c) * half, 128), half)], (csend, crecv), i, partner)
-        sent[2 * i].wait()
-        sent[2 * i + 1].wait_send()
-
-
-def gather_weights(ssm, att, gu, dn):
+    cots.finish()
+
+
+def forward_and_gather(proj, consts, cot, shards):
+    seq_len = proj.shape[0]
+    chunks = seq_len // CHUNK
     total = 4 * ARRAY_SENDS
+    ssm, att, gu, dn = shards
     outs = pl.pallas_call(
-        gather_kernel,
-        name="gather_weights",
+        forward_kernel,
+        name="mixer_forward_and_gather",
         out_shape=(
+            jax.ShapeDtypeStruct((seq_len, XW), BF),
+            jax.ShapeDtypeStruct((seq_len, QW), BF),
+            jax.ShapeDtypeStruct((seq_len, 128), F32),
+            jax.ShapeDtypeStruct((seq_len, XW), F32),
+            jax.ShapeDtypeStruct((chunks, NS, XW), F32),
+            jax.ShapeDtypeStruct((4,) + cot.shape[1:], BF),
             jax.ShapeDtypeStruct((4, ssm.shape[0], 2 * ssm.shape[1]), BF),
             jax.ShapeDtypeStruct((4, att.shape[0], 2 * att.shape[1]), BF),
             jax.ShapeDtypeStruct((8,) + gu.shape, BF),
             jax.ShapeDtypeStruct((8,) + dn.shape, BF),
-            jax.ShapeDtypeStruct((8,) + ssm.shape, BF),
-            jax.ShapeDtypeStruct((8,) + att.shape, BF),
         ),
-        in_specs=any_specs(4),
-        out_specs=tuple(any_specs(6)),
+        in_specs=whole(13),
+        out_specs=tuple(whole(5) + any_specs(5)),
         scratch_shapes=[
+            VM((NS, XW), F32),
+            VM((8,) + ssm.shape, BF),
+            VM((8,) + att.shape, BF),
             pltpu.SemaphoreType.DMA((total,)),
             pltpu.SemaphoreType.DMA((total,)),
-            pltpu.SemaphoreType.DMA((2,)),
-            pltpu.SemaphoreType.DMA((2,)),
-            pltpu.SemaphoreType.DMA((6,)),
+            pltpu.SemaphoreType.DMA((5,)),
+            pltpu.SemaphoreType.DMA((5,)),
+            pltpu.SemaphoreType.DMA((7,)),
         ],
-        compiler_params=pltpu.CompilerParams(collective_id=1, has_side_effects=True),
-    )(ssm, att, gu, dn)
-    return [v.reshape(-1, v.shape[-1]) for v in outs[:4]]
+        compiler_params=pltpu.CompilerParams(collective_id=1, has_side_effects=True, vmem_limit_bytes=56 * MIB),
+    )(proj, *consts, cot, ssm, att, gu, dn)
+    return outs[:5], outs[5].reshape(seq_len, -1), [v.reshape(-1, v.shape[-1]) for v in outs[6:]]
+
+
+def plain_forward_kernel(proj, cosine, sine, segc, segr, par, spread, wide, gated, attn, lse, y_own, states, state):
+    tick = Ticker([], 1)
+    attention_forward(proj, cosine, sine, segc, segr, attn, lse, tick)
+    scan_forward(proj, segc, segr, par, spread, wide, gated, y_own, states, state, tick)
+
+
+def mixer_forward(proj, consts):
+    seq_len = proj.shape[0]
+    return pl.pallas_call(
+        plain_forward_kernel,
+        name="mixer_forward",
+        out_shape=(
+            jax.ShapeDtypeStruct((seq_len, XW), BF),
+            jax.ShapeDtypeStruct((seq_len, QW), BF),
+            jax.ShapeDtypeStruct((seq_len, 128), F32),
+            jax.ShapeDtypeStruct((seq_len, XW), F32),
+            jax.ShapeDtypeStruct((seq_len // CHUNK, NS, XW), F32),
+        ),
+        in_specs=whole(8),
+        out_specs=tuple(whole(5)),
+        scratch_shapes=[VM((NS, XW), F32)],
+        compiler_params=pltpu.CompilerParams(vmem_limit_bytes=56 * MIB),
+    )(proj, *consts)
 
 
 def pair_kernel(blocks, part, got, sems_out, sems_in):
@@ -619,7 +721,7 @@
         columns_kernel,
         name="swap_columns",
         out_shape=tuple(jax.ShapeDtypeStruct((8, v.shape[1], v.shape[2] // 2), BF) for v in args),
-        in_specs=any_specs(2),
+        in_specs=whole(2),
         out_specs=tuple(any_specs(2)),
         scratch_shapes=[pltpu.SemaphoreType.DMA((2,))] * 3,
         compiler_params=pltpu.CompilerParams(collective_id=5, has_side_effects=True),
@@ -627,8 +729,6 @@
 
 
 class Reduce:
-    VIA_X = (0, 1)
-
     def __init__(self, part, out, far, near_x, near_y, deep, sems, base):
         self.part, self.out, self.far, self.near_x, self.near_y, self.deep = part, out, far, near_x, near_y, deep
         self.sems, self.base = sems, base
@@ -649,36 +749,41 @@
     def start(self):
         for r in (1, 2, 3, 0):
             far = self.piece(r, 1 - self.x, self.other)
-            self.push(r, far, self.far.at[r], self.xpeer if r in self.VIA_X else self.ypeer)
-        for r in (1, 2, 3, 0):
-            if r in self.VIA_X:
-                self.push(4 + r, self.piece(r, 1 - self.x, self.mine), self.near_x.at[r], self.xpeer)
-            else:
-                self.push(8 + r, self.piece(r, self.x, self.other), self.near_y.at[r], self.ypeer)
+            self.push(r, far, self.far.at[r], self.ypeer if r == 1 else self.xpeer)
+        self.push(9, self.piece(1, self.x, self.other), self.near_y.at[1], self.ypeer)
+        for r in (2, 3):
+            self.push(4 + r, self.piece(r, 1 - self.x, self.mine), self.near_x.at[r], self.xpeer)
 
     def relay(self, r):
         landed(self.far.at[r], self.sems, self.base + r, self.xpeer)
-        own = self.piece(r, self.x, self.other) if r in self.VIA_X else self.piece(r, 1 - self.x, self.mine)
+        own = self.piece(r, 1 - self.x, self.mine) if r == 1 else self.piece(r, self.x, self.other)
         self.far[r] = (own[...].astype(F32) + self.far[r].astype(F32)).astype(BF)
-        if r in self.VIA_X:
+        if r == 1:
+            self.push(5, self.far.at[1], self.near_x.at[1], device(self.z ^ 1, self.x, self.y, self.c))
+        else:
             self.push(8 + r, self.far.at[r], self.near_y.at[r], self.ypeer)
-        else:
-            self.push(4 + r, self.far.at[r], self.near_x.at[r], self.xpeer)
+
+    def cross(self):
+        landed(self.near_x.at[1], self.sems, self.base + 5, self.xpeer)
+        own = self.piece(0, 1 - self.x, self.mine)[...].astype(F32)
+        self.near_x[1] = (own + self.near_x[1].astype(F32)).astype(BF)
+        self.push(4, self.near_x.at[1], self.near_x.at[0], self.xpeer)
 
     def root(self, r):
-        landed(self.near_x.at[r], self.sems, self.base + 4 + r, self.xpeer)
         landed(self.near_y.at[r], self.sems, self.base + 8 + r, self.ypeer)
-        own = self.piece(r, self.x, self.mine)[...].astype(F32)
-        total = own + (self.near_x[r].astype(F32) + self.near_y[r].astype(F32))
-        self.near_x[r] = total.astype(BF)
+        total = self.piece(r, self.x, self.mine)[...].astype(F32) + self.near_y[r].astype(F32)
+        if r != 1:
+            landed(self.near_x.at[r], self.sems, self.base + 4 + r, self.xpeer)
+            total = total + self.near_x[r].astype(F32)
+        self.near_y[r] = total.astype(BF)
         if r:
             target = device(self.z ^ r, self.x, self.y, self.c)
-            self.push(11 + r, self.near_x.at[r], self.deep.at[r - 1], target)
+            self.push(11 + r, self.near_y.at[r], self.deep.at[r - 1], target)
 
     def total(self, partner):
         for r in (1, 2, 3):
             landed(self.deep.at[r - 1], self.sems, self.base + 11 + r, self.xpeer)
-        total = self.near_x[0].astype(F32) + self.deep[0].astype(F32)
+        total = self.near_y[0].astype(F32) + self.deep[0].astype(F32)
         total = total + (self.deep[1].astype(F32) + self.deep[2].astype(F32))
         self.out[self.c, self.mine] = total.astype(BF)
         ref = self.out.at[self.c, self.mine]
@@ -698,78 +803,124 @@
 
 
 REDUCE_SENDS = 18
-N_REDUCED = 5
-
-
-def reduce_kernel(*refs):
-    parts, refs = refs[:N_REDUCED], refs[N_REDUCED:]
-    out_rows, gx, refs = refs[0], refs[1], refs[2:]
-    reduced, refs = refs[:N_REDUCED], refs[N_REDUCED:]
-    output, returned, refs = refs[0], refs[1], refs[2:]
-    buffers, refs = [refs[4 * i : 4 * i + 4] for i in range(N_REDUCED)], refs[4 * N_REDUCED :]
-    rsend, rrecv, dsend, drecv, local = refs
-    z, x, y, c = place()
-    own = 2 * z + x
-    slot = 2 * own + y
-    partner = device(z, x, y, 1 - c)
-    ypeer = device(z, x, 1 - y, c)
-    others = [(r, i, j) for r in range(4) for i in range(2) for j in range(2) if r or i or j]
-    targets = [device(z ^ r, x ^ i, y ^ j, c) for r, i, j in others]
-    greet(targets + [partner])
-    sums = [Reduce(p, o, *b, (rsend, rrecv), REDUCE_SENDS * k) for k, (p, o, b) in enumerate(zip(parts, reduced, buffers))]
-    for s in sums:
-        s.start()
-    columns = lambda d: pl.ds(pl.multiple_of(d * 128, 128), 128)
-    sems = (dsend, drecv)
-    sent = [send(out_rows.at[1 - y], output.at[y], sems, 15, ypeer)]
-    here = [
-        pltpu.make_async_copy(out_rows.at[y], output.at[y], local.at[0]),
-        pltpu.make_async_copy(gx.at[y, :, columns(own)], returned.at[slot], local.at[1]),
-    ]
-    for copy in here:
-        copy.start()
-    for k, (r, i, j) in enumerate(others):
-        d = 2 * (z ^ r) + (x ^ i)
-        sent.append(send(gx.at[y ^ j, :, columns(d)], returned.at[slot], sems, k, targets[k]))
-    for s in sums:
-        for r in (1, 2, 3, 0):
-            s.relay(r)
-    for s in sums:
-        for r in (1, 2, 3, 0):
-            s.root(r)
-    for s in sums:
-        s.total(partner)
-    for s in sums:
-        s.spread(partner)
-    for s in sums:
-        s.finish(partner)
-    for k, (r, i, j) in enumerate(others):
-        landed(returned.at[2 * (2 * (z ^ r) + (x ^ i)) + (y ^ j)], sems, k, targets[k])
-    landed(output.at[1 - y], sems, 15, ypeer)
-    for copy in sent:
-        copy.wait_send()
-    for copy in here:
-        copy.wait()
-
-
-def reduce_all(parts, out_rows, gx):
-    outs = [jax.ShapeDtypeStruct((2,) + p.shape[1:], BF) for p in parts]
-    outs += [jax.ShapeDtypeStruct(out_rows.shape, BF), jax.ShapeDtypeStruct((16, gx.shape[1], 128), BF)]
+
+
+def reduce_buffers(parts):
     scratch = []
     for p in parts:
         half = (p.shape[1] // 2, p.shape[2])
         scratch += [VM((4,) + half, BF)] * 3 + [VM((3,) + half, BF)]
     total = REDUCE_SENDS * len(parts)
-    scratch += [pltpu.SemaphoreType.DMA((n,)) for n in (total, total, 16, 16, 2)]
+    return scratch + [pltpu.SemaphoreType.DMA((total,))] * 2
+
+
+def backward_kernel(*refs):
+    proj, cosine, sine, segc, segr, par, spread, wide, attn, lse, y_own, states, ggated, gattn, *refs = refs
+    parts, out_rows, (gproj, gpar), reduced, output, refs = refs[:4], refs[4], refs[5:7], refs[7:11], refs[11], refs[12:]
+    gkv, gstate, *refs = refs
+    buffers, (rsend, rrecv, osend, orecv, local) = [refs[4 * i : 4 * i + 4] for i in range(4)], refs[16:]
+    z, x, y, c = place()
+    partner = device(z, x, y, 1 - c)
+    ypeer = device(z, x, 1 - y, c)
+    greet(chip_peers())
+    sums = [Reduce(p, o, *b, (rsend, rrecv), REDUCE_SENDS * k) for k, (p, o, b) in enumerate(zip(parts, reduced, buffers))]
+    sums[0].start()
+    sent = send(out_rows.at[1 - y], output.at[y], (osend, orecv), 0, ypeer)
+    here = pltpu.make_async_copy(out_rows.at[y], output.at[y], local.at[0])
+    here.start()
+    ticker = Ticker(reduce_steps(sums, partner), 40)
+    attention_backward(proj, cosine, sine, segc, segr, attn, lse, gattn, gproj, gkv, ticker)
+    scan_backward(proj, segc, segr, par, spread, wide, y_own, states, ggated, gproj, gpar, gstate, ticker)
+    ticker.drain()
+    for s in sums:
+        s.finish(partner)
+    landed(output.at[1 - y], (osend, orecv), 0, ypeer)
+    sent.wait_send()
+    here.wait()
+
+
+def backward_and_reduce(proj, consts, saved, ggated, gattn, parts, out_rows):
+    seq_len = proj.shape[0]
+    outs = [jax.ShapeDtypeStruct((seq_len, COLS), BF), jax.ShapeDtypeStruct((8, 128), F32)]
+    outs += [jax.ShapeDtypeStruct((2,) + p.shape[1:], BF) for p in parts]
+    outs += [jax.ShapeDtypeStruct(out_rows.shape, BF)]
+    scratch = [VM((seq_len, 256), F32), VM((NS, XW), F32)] + reduce_buffers(parts)
+    scratch += [pltpu.SemaphoreType.DMA((1,))] * 3
     return pl.pallas_call(
-        reduce_kernel,
+        backward_kernel,
+        name="mixer_backward_and_reduce",
+        out_shape=tuple(outs),
+        in_specs=whole(14 + len(parts) + 1),
+        out_specs=tuple(whole(2 + len(parts)) + any_specs(1)),
+        scratch_shapes=scratch,
+        compiler_params=pltpu.CompilerParams(collective_id=6, has_side_effects=True, vmem_limit_bytes=62 * MIB),
+    )(proj, *consts, *saved, ggated, gattn, *parts, out_rows)
+
+
+def plain_backward_kernel(proj, cosine, sine, segc, segr, par, spread, wide, attn, lse, y_own, states, ggated, gattn, gproj, gpar, gkv, gstate):
+    tick = Ticker([], 1)
+    attention_backward(proj, cosine, sine, segc, segr, attn, lse, gattn, gproj, gkv, tick)
+    scan_backward(proj, segc, segr, par, spread, wide, y_own, states, ggated, gproj, gpar, gstate, tick)
+
+
+def mixer_backward(proj, consts, saved, ggated, gattn):
+    seq_len = proj.shape[0]
+    return pl.pallas_call(
+        plain_backward_kernel,
+        name="mixer_backward",
+        out_shape=(
+            jax.ShapeDtypeStruct((seq_len, COLS), BF),
+            jax.ShapeDtypeStruct((8, 128), F32),
+        ),
+        in_specs=whole(14),
+        out_specs=tuple(whole(2)),
+        scratch_shapes=[VM((seq_len, 256), F32), VM((NS, XW), F32)],
+        compiler_params=pltpu.CompilerParams(vmem_limit_bytes=56 * MIB),
+    )(proj, *consts, *saved, ggated, gattn)
+
+
+def end_kernel(part, gx, reduced, returned, far, near_x, near_y, deep, rsend, rrecv, dsend, drecv, local):
+    z, x, y, c = place()
+    own = 2 * z + x
+    slot = 2 * own + y
+    partner = device(z, x, y, 1 - c)
+    others = [(r, i, j) for r in range(4) for i in range(2) for j in range(2) if r or i or j]
+    targets = [device(z ^ r, x ^ i, y ^ j, c) for r, i, j in others]
+    greet(targets + [partner])
+    sums = [Reduce(part, reduced, far, near_x, near_y, deep, (rsend, rrecv), 0)]
+    sums[0].start()
+    columns = lambda d: pl.ds(pl.multiple_of(d * 128, 128), 128)
+    sems = (dsend, drecv)
+    here = pltpu.make_async_copy(gx.at[y, :, columns(own)], returned.at[slot], local.at[0])
+    here.start()
+    sent = []
+    for k, (r, i, j) in enumerate(others):
+        d = 2 * (z ^ r) + (x ^ i)
+        sent.append(send(gx.at[y ^ j, :, columns(d)], returned.at[slot], sems, k, targets[k]))
+    for step in reduce_steps(sums, partner):
+        step()
+    for s in sums:
+        s.finish(partner)
+    for k, (r, i, j) in enumerate(others):
+        landed(returned.at[2 * (2 * (z ^ r) + (x ^ i)) + (y ^ j)], sems, k, targets[k])
+    for copy in sent:
+        copy.wait_send()
+    here.wait()
+
+
+def end_transfers(part, gx):
+    return pl.pallas_call(
+        end_kernel,
         name="reduce_and_return",
-        out_shape=tuple(outs),
-        in_specs=whole(len(parts)) + any_specs(2),
-        out_specs=tuple(whole(len(parts)) + any_specs(2)),
-        scratch_shapes=scratch,
+        out_shape=(
+            jax.ShapeDtypeStruct((2,) + part.shape[1:], BF),
+            jax.ShapeDtypeStruct((16, gx.shape[1], 128), BF),
+        ),
+        in_specs=whole(2),
+        out_specs=tuple(whole(1) + any_specs(1)),
+        scratch_shapes=reduce_buffers([part]) + [pltpu.SemaphoreType.DMA((n,)) for n in (15, 15, 1)],
         compiler_params=pltpu.CompilerParams(collective_id=4, has_side_effects=True, vmem_limit_bytes=60 * MIB),
-    )(*parts, out_rows, gx)
+    )(part, gx)
 
 
 def plain_start(dealt, cot, w, y):
@@ -866,10 +1017,8 @@
 
     dealt = jnp.take(tokens, deal_order, axis=0)
     if fast:
-        rows, w_in, cots = start_transfers(dealt, cot, w_in)
-        rows, cots = rows.reshape(seq_len, width), cots.reshape(seq_len, width)
-        w_in = w_in.reshape(width, COLS)
-        w_ssm, w_att, w_gu, w_dn = gather_weights(w_ssm, w_att, w_gu, w_dn)
+        rows, w_in = start_transfers(dealt, w_in)
+        rows, w_in = rows.reshape(seq_len, width), w_in.reshape(width, COLS)
         pair = pair_swap
     else:
         rows, w_in, cots = plain_start(dealt, cot, w_in, y)
@@ -901,7 +1050,12 @@
     unit_in, scale_in = rms_parts(x)
     normed = low(unit_in * gain_in)
     proj = low(dot(normed, w_in))
-    gated, attn, lse, y_own, states = mixer_forward(proj, consts)
+    if fast:
+        (gated, *saved), cots, weights = forward_and_gather(proj, consts, cot, (w_ssm, w_att, w_gu, w_dn))
+        w_ssm, w_att, w_gu, w_dn = weights
+    else:
+        gated, *saved = mixer_forward(proj, consts)
+    attn = saved[0]
     part = low(dot(gated, w_ssm) + dot(attn, w_att))
     middle = x + (part.astype(F32) + pair(part).astype(F32))
     unit_ffn, scale_ffn = rms_parts(middle)
@@ -928,7 +1082,12 @@
     g_attn = low(dot(g_branch, w_att, ((1,), (1,))))
     grad_ssm = low(dot(gated, g_branch, ((0,), (0,))))
     grad_att = low(dot(attn, g_branch, ((0,), (0,))))
-    g_proj, g_par = mixer_backward(proj, consts, attn, lse, y_own, states, g_gated, g_attn)
+    by_block = lambda v: v.reshape(groups, -1, v.shape[-1])
+    if fast:
+        parts = (by_block(grad_dn), by_block(grad_gu)) + tuple(by_block(v) for v in swap_columns(grad_ssm, grad_att))
+        g_proj, g_par, *reduced, output = backward_and_reduce(proj, consts, saved, g_gated, g_attn, parts, out_rows)
+    else:
+        g_proj, g_par = mixer_backward(proj, consts, saved, g_gated, g_attn)
     grad_in = dot(normed, g_proj, ((0,), (0,)))
     part = low(dot(g_proj, w_in, ((1,), (1,)))).reshape(4, span, width)
     g_h1 = low(by_core(part).astype(F32) + swap_rows(part).astype(F32)).astype(F32)
@@ -939,20 +1098,16 @@
     extra = jnp.concatenate([grad_gain_in[:, None], grad_gain_ffn[:, None], head_grads], axis=1)
     grad_in = low(lax.dynamic_update_slice(grad_in, extra, (0, T0 + CHIP_HEADS)))
 
-    by_block = lambda v: v.reshape(groups, -1, v.shape[-1])
     if fast:
-        parts = (by_block(grad_in), by_block(grad_gu), by_block(grad_dn))
-        parts += tuple(by_block(v) for v in swap_columns(grad_ssm, grad_att))
-        *reduced, output, returned = reduce_all(parts, out_rows, g_x)
-        reduced = [v.astype(F32) for v in reduced]
+        r_in, returned = end_transfers(by_block(grad_in), g_x)
+        r_in, r_dn, r_gu, r_ssm, r_att = [v.astype(F32) for v in (r_in, *reduced)]
     else:
-        parts = [by_block(grad_in), by_block(grad_gu), by_block(grad_dn)]
+        parts = [by_block(grad_in), by_block(grad_dn), by_block(grad_gu)]
         for v in (grad_ssm, grad_att):
             both = jnp.stack([v, plain_pair(v)])
             both = jnp.where(c == 0, both, both[::-1]).reshape(-1, width)
             parts.append(by_block(cut(both, width // 2 * c, width // 2)))
-        reduced, output, returned = plain_reduce(parts, out_rows, g_x, y, c)
-    r_in, r_gu, r_dn, r_ssm, r_att = reduced
+        (r_in, r_dn, r_gu, r_ssm, r_att), output, returned = plain_reduce(parts, out_rows, g_x, y, c)
     both = lambda start, size: [r_in[0, :, start : start + size], r_in[1, :, start : start + size]]
     grad_in_proj = jnp.concatenate(
         both(Z0, XW)

time: 643 us -> 535 us (0.83)
  Pallas kernels: 466 us -> 359 us
    pallas_call x4 -> x3, Pallas kernels: 337 us -> 270 us  [the longest x1 111 us: backward_and_reduce(): pl.pallas_call(backward_kernel, name='mixer_backward_and_reduce', out_sha...]
    pallas_call x1, Pallas kernels: 33.3 us -> 4.36 us  [swap_columns(): pl.pallas_call(columns_kernel, name='swap_columns', out_shape=tuple((jax....]
where the time goes in v2:
time: 535 us; the launch traced here: 526 us
  Pallas kernels  359 us (67%)
  matrix products  76.8 us (14%)
  local copies, waits for them, and re-layouts  46 us (9%)
  other arithmetic  40.5 us (8%)
    pallas_call x1, Pallas kernels, backward_and_reduce(): pl.pallas_call(backward_kernel, name='mixer_backward_and_reduce', out_sha...  111 us
    pallas_call x1, Pallas kernels, forward_and_gather(): pl.pallas_call(forward_kernel, name='mixer_forward_and_gather', out_shape...  81.3 us
    pallas_call x1, Pallas kernels, end_transfers(): pl.pallas_call(end_kernel, name='reduce_and_return', out_shape=(jax.Shape...  77.2 us
    dot_general x15, matrix products, dot(): lax.dot_general(a, b, (dims, ((), ())), precision=precision, preferred_el...  76.8 us
    pallas_call x1, Pallas kernels, start_transfers(): pl.pallas_call(start_kernel, name='deal_and_gather', out_shape=(jax.Shape...  67.5 us
    pallas_call x4, Pallas kernels, pair_swap(): pl.pallas_call(functools.partial(pair_kernel, blocks), name='pair_swap_ro...  17.8 us
    convert_element_type x4, other arithmetic, low(): return v.astype(BF)  11 us

profile of v2, /device:TPU:9, one launch (start us, length us, event | category | flops | bytes accessed | tf_op | source)
XLA Modules:
  0.0 526.1 jit_solution(11977411506569499030)
XLA Ops:
  0.7 2.0 sort.17
  2.7 1.2 compare_select_fusion
  3.9 0.7 gather_fusion
  5.2 1.1 broadcast_select_fusion.1.dealt
  7.0 1.0 concatenate.29.w
  7.9 67.5 %deal_and_gather.1 = (bf16[4,256,1024]{2,1,0:T(8,128)(2,1)}, bf16[8,128,2304]{2,1,0:T(8,128)(2,1)}) custom-call(bf16[16,256,128]{2,1,0:T(8,128)(2,1)} %broadcast_select_fusion.1.dealt, bf16[128,2304]{1,0:T(8,128)(2,1)} %concatenate.29.w), custom_call_target="tpu_custom_call" | custom-call | tf_op jit(solution)/shard_map/deal_and_gather/pallas_call | solution.py:509
  75.5 2.2 slice_convert_fusion
  78.9 1.3 copy-done.23
  80.2 6.7 %convolution_convert_fusion.refs_0_ = bf16[1024,2304]{1,0:T(8,128)(2,1)} fusion(bf16[1024,1024]{1,0:T(8,128)(2,1)S(1)} %bitcast.194, bf16[1024,2304]{1,0:T(8,128)(2,1)S(1)} %bitcast.208), kind=kOutput, calls=%fused_computation.2 | convolution fusion | flops 4834197504 | bytes 11534336 | tf_op jit(solution)/shard_map/dot_general | solution.py:36
  87.6 1.0 copy.100.refs_1_
  88.6 1.0 copy.101.refs_2_
  89.6 1.2 dynamic_slice.77
  93.3 1.0 broadcast_in_dim.30.refs_3_
  94.9 0.7 negate_bitcast_fusion
  95.9 0.8 compare_convert_fusion.refs_6_
  98.8 1.5 constant_dynamic-slice_fusion.3.refs_10_
  100.3 1.8 reshape.349
  102.1 3.1 dynamic-slice_reduce_fusion
  105.2 0.9 copy.140
  106.1 1.7 constant_dynamic-slice_fusion.2.refs_12_
  107.8 81.3 %mixer_forward_and_gather.1 = (bf16[1024,768]{1,0:T(8,128)(2,1)}, bf16[1024,256]{1,0:T(8,128)(2,1)}, f32[1024,128]{1,0:T(8,128)}, f32[1024,768]{1,0:T(8,128)}, f...) custom-call(bf16[1024,2304]{1,0:T(8,128)(2,1)} %convolution_convert_, ...), custom_call_target="tpu_custom_call" | custom-call | tf_op jit(solution)/shard_map/mixer_forward_and_gather/pallas_call | solution.py:618
  189.2 3.8 fusion.38
  192.9 2.1 add_convert_fusion.1.part
  195.0 6.0 %pair_swap.2 = bf16[1024,1024]{1,0:T(8,128)(2,1)} custom-call(bf16[1024,1024]{1,0:T(8,128)(2,1)} %add_convert_fusion.1.part), custom_call_target="tpu_custom_call" | custom-call | tf_op jit(solution)/shard_map/pair_swap/pallas_call | solution.py:690
  201.1 6.5 %multiply_reduce_fusion = (f32[1024]{0:T(1024)S(1)}, f32[1024,1024]{1,0:T(8,128)}, bf16[1024,1024]{1,0:T(8,128)(2,1)}) fusion(bf16[1024,1024]{1,0:T(8,128)(2,1)} %pair_swap.2, bf16[1024,1024]{1,0:T(8,128)(2,1)} %add_convert_fusion.1.part, bf16[4,256,1024]{2,1,0:T(8,128)(2,1)S(1)} %copy-done.3, f32[1024]{0:T(1024)S(1)} %bitcast.203, f32[1024]{0:T(1024)S(1)} %bitcast.214), kind=kLoop, calls=%fused_computation.27 | loop fusion | flops 10484736 | bytes 12595200 | tf_op jit(solution)/shard_map/reduce_sum | solution.py:965
  207.7 8.0 %convert_convert_fusion = f32[1024,2048]{0,1:T(8,128)S(1)} fusion(bf16[1024,2048]{1,0:T(8,128)(2,1)} %bitcast.220, f32[1024,1024]{1,0:T(8,128)} %get-tuple-element.122, f32[1024]{0:T(1024)S(1)} %bitcast.209, f32[1024]{0:T(1024)S(1)} %add_rsqrt_fusion), kind=kOutput, calls=%fused_computation.25 | convolution fusion | flops 4302307328 | bytes 16785408 | tf_op jit(solution)/shard_map/dot_general | solution.py:36
  215.8 5.3 fusion.6
  221.0 1.3 copy-done.38
  223.0 5.8 %fusion.23.part = bf16[1024,1024]{1,0:T(8,128)(2,1)} fusion(bf16[1024,2048]{1,0:T(8,128)(2,1)S(1)} %bitcast.221, bf16[1024,1024]{0,1:T(8,128)(2,1)S(1)} %get-tuple-element.124, bf16[1024,1024]{0,1:T(8,128)(2,1)S(1)} %get-tuple-element.123), kind=kOutput, calls=%fused_computation.50 | convolution fusion | flops 4304404480 | bytes 10485760 | tf_op jit(solution)/shard_map/dot_general | solution.py:36
  228.8 4.5 pair_swap.3
  233.4 4.4 fusion.8
  238.7 3.3 fusion.35
  242.0 3.0 convolution_convert_fusion.7.refs_12_
  245.0 1.5 convolution_convert_fusion.9.refs_13_
  246.6 3.8 convolution_convert_fusion.4
  250.4 8.2 %convolution_convert_fusion.1 = bf16[1024,2048]{1,0:T(8,128)(2,1)} fusion(bf16[1024,1024]{0,1:T(8,128)(2,1)S(1)} %copy-done.41, bf16[1024,1024]{0,1:T(8,128)(2,1)S(1)} %copy-done.39, f32[1024,1024]{1,0:T(8,128)S(1)} %copy-done.2, f32[1024]{0:T(1024)S(1)} %bitcast.212, f32[1024]{0:T(1024)S(1)} %add_rsqrt_fusion), kind=kOutput, calls=%fused_computation.31 | convolution fusion | flops 4308598784 | bytes 12591104 | tf_op jit(solution)/shard_map/dot_general | solution.py:36
  258.6 3.0 convolution_convert_fusion.6
  261.7 1.5 convolution_convert_fusion.8
  263.2 4.4 swap_columns.1
  267.6 5.3 %convolution_convert_fusion.3 = bf16[1024,1024]{1,0:T(8,128)(2,1)} fusion(bf16[1024,1024]{0,1:T(8,128)(2,1)} %get-tuple-element.125, bf16[1024,1024]{1,0:T(8,128)(2,1)S(1)} %bitcast.223), kind=kOutput, calls=%fused_computation.52 | convolution fusion | flops 2148532224 | bytes 6291456 | tf_op jit(solution)/shard_map/dot_general | solution.py:36
  272.8 3.0 pair_swap_rows.2
  275.9 3.4 fusion.21.refs_18_
  279.3 111.2 %mixer_backward_and_reduce.1 = (bf16[1024,2304]{1,0:T(8,128)(2,1)}, f32[8,128]{1,0:T(8,128)}, bf16[2,128,1024]{2,1,0:T(8,128)(2,1)}, bf16[2,128,2048]{2,1,0:T(8,...) custom-call(bf16[1024,2304]{1,0:T(8,128)(2,1)} %convolution_convert_fusion.refs_, ...), custom_call_target="tpu_custom_call" | custom-call | tf_op jit(solution)/shard_map/mixer_backward_and_reduce/pallas_call | solution.py:849
  390.5 9.5 %fusion.39 = bf16[1024,2304]{1,0:T(8,128)(2,1)} fusion(bf16[1024,1024]{1,0:T(8,128)(2,1)} %get-tuple-element.143, bf16[1024,2304]{1,0:T(8,128)(2,1)} %get-tuple-element.77), kind=kOutput, calls=%fused_computation.150 | convolution fusion | flops 4831838208 | bytes 11534336 | tf_op jit(solution)/shard_map/dot_general | solution.py:36
  400.7 9.3 %convolution_convert_fusion.2 = bf16[1024,1024]{1,0:T(8,128)(2,1)} fusion(bf16[1024,2304]{1,0:T(8,128)(2,1)} %get-tuple-element.77, bf16[1024,2304]{1,0:T(8,128)(2,1)} %bitcast.207), kind=kOutput, calls=%fused_computation.51 | convolution fusion | flops 4832886784 | bytes 11534336 | tf_op jit(solution)/shard_map/dot_general | solution.py:36
  410.0 4.2 pair_swap_rows.3
  414.7 1.1 copy-done.8
  416.1 0.8 fusion.15
  417.0 1.1 copy-done.7
  418.3 3.2 dynamic_update_slice.3
  421.5 3.8 fusion.18.gx
  425.3 77.2 %reduce_and_return.1 = (bf16[2,128,2304]{2,1,0:T(8,128)(2,1)}, bf16[16,256,128]{2,1,0:T(8,128)(2,1)}) custom-call(bf16[8,128,2304]{2,1,0:T(8,128)(2,1)} %bitcast.184, bf16[2,256,1024]{2,1,0:T(8,128)(2,1)} %fusion.18.gx), custom_call_target="tpu_custom_call" | custom-call | tf_op jit(solution)/shard_map/reduce_and_return/pallas_call | solution.py:912
  502.5 2.0 gather_fusion.1
  504.5 1.1 broadcast_select_fusion
  507.1 1.0 slice_bitcast_fusion.4
  508.2 0.8 slice_bitcast_fusion.14
  508.9 3.3 concatenate.33
  513.1 0.8 slice.205
  514.5 1.1 convert_element_type.245
  515.7 0.9 pad_maximum_fusion.6
  518.4 1.6 copy.111
  520.1 2.7 reshape.366
  522.7 2.2 bitcast_convert_fusion
  525.0 1.0 copy.145
  (153 shorter events, 14.8 us)
Async XLA Ops:
  0.6 3.2 copy-start
  0.7 4.0 copy-start.29
  3.8 2.5 copy-start.20
  4.6 1.9 copy-start.25
  4.6 2.0 copy-start.30
  4.6 2.2 copy-start.31
  75.5 2.4 copy-start.3
  77.9 2.4 copy-start.23
  87.5 5.3 %copy-start.27 = (s32[16,4]{0,1:T(4,128)S(1)}, s32[16,4]{0,1:T(4,128)}, u32[]{:S(2)}) copy-start(s32[16,4]{0,1:T(4,128)} %param.23) | copy-start | bytes 772
  87.6 10.6 %copy-start.22 = (bf16[192,1024]{1,0:T(8,128)(2,1)S(1)}, bf16[192,1024]{1,0:T(8,128)(2,1)}, u32[]{:S(2)}) copy-start(bf16[192,1024]{1,0:T(8,128)(2,1)} %param.31) | copy-start | bytes 1179652
  95.9 9.3 %copy-start.24 = (f32[8,128]{1,0:T(8,128)}, f32[8,128]{1,0:T(8,128)S(1)}, u32[]{:S(2)}) copy-start(f32[8,128]{1,0:T(8,128)S(1)} %scatter.9.refs_5_) | copy-start | bytes 12292
  189.1 3.8 copy-start.10
  189.2 3.8 copy-start.18
  201.0 6.5 %copy-start.14 = (f32[1024,1]{1,0:T(8,128)S(1)}, f32[1024,1]{1,0:T(8,128)}, u32[]{:S(2)}) copy-start(f32[1024,1]{1,0:T(8,128)} %get-tuple-element.126) | copy-start | bytes 12292
  207.7 8.0 %copy-start.12 = (bf16[4,256,1024]{2,1,0:T(8,128)(2,1)S(1)}, bf16[4,256,1024]{2,1,0:T(8,128)(2,1)}, u32[]{:S(2)}) copy-start(bf16[4,256,1024]{2,1,0:T(8,128)(2,1)} %get-tuple-element.68) | copy-start | bytes 6291460
  207.7 8.0 %copy-start.33 = (bf16[8,128,1024]{2,1,0:T(8,128)(2,1)S(1)}, bf16[8,128,1024]{2,1,0:T(8,128)(2,1)}, u32[]{:S(2)}) copy-start(bf16[8,128,1024]{2,1,0:T(8,128)(2,1)} %get-tuple-element.72) | copy-start | bytes 6291460
  215.8 7.3 %copy-start.32 = (bf16[8,128,2048]{2,1,0:T(8,128)(2,1)S(1)}, bf16[8,128,2048]{2,1,0:T(8,128)(2,1)}, u32[]{:S(2)}) copy-start(bf16[8,128,2048]{2,1,0:T(8,128)(2,1)} %get-tuple-element.73) | copy-start | bytes 12582916
  221.0 1.3 copy-start.38
  221.0 2.0 copy-start.40
  228.8 4.5 copy-start.5
  233.4 4.4 copy-start.2
  233.4 4.7 copy-start.6
  233.4 5.3 %copy-start.13 = (bf16[4,256,1024]{2,1,0:T(8,128)(2,1)S(1)}, bf16[4,256,1024]{2,1,0:T(8,128)(2,1)}, u32[]{:S(2)}) copy-start(bf16[4,256,1024]{2,1,0:T(8,128)(2,1)} %get-tuple-element.68) | copy-start | bytes 6291460
  238.7 3.3 copy-start.36
  242.0 3.0 copy-start.19
  245.0 1.6 copy-start.37
  246.6 3.8 copy-start.39
  246.6 3.8 copy-start.41
  250.4 8.2 %copy-start.35 = (bf16[1024,768]{1,0:T(8,128)(2,1)S(1)}, bf16[1024,768]{1,0:T(8,128)(2,1)}, u32[]{:S(2)}) copy-start(bf16[1024,768]{1,0:T(8,128)(2,1)} %get-tuple-element.69) | copy-start | bytes 4718596
  261.7 5.9 %copy-start.34 = (bf16[8,128,1024]{2,1,0:T(8,128)(2,1)S(1)}, bf16[8,128,1024]{2,1,0:T(8,128)(2,1)}, u32[]{:S(2)}) copy-start(bf16[8,128,1024]{2,1,0:T(8,128)(2,1)} %get-tuple-element.72) | copy-start | bytes 6291460
  272.8 3.0 copy-start.9
  410.0 4.2 copy-start.4
  414.3 1.6 copy-start.8
  414.3 1.8 copy-start.11
  416.1 1.9 copy-start.7
  425.3 77.2 %copy-start.28 = (s32[16]{0:T(128)S(1)}, s32[16]{0:T(128)}, u32[]{:S(2)}) copy-start(s32[16]{0:T(128)} %get-tuple-element.162) | copy-start | bytes 196
  502.5 2.0 copy-start.26
  504.5 1.6 copy-start.15
  514.5 2.1 copy-start.21
  515.7 1.8 copy-start.16
  520.0 5.9 %copy-start.1 = (bf16[16,256,128]{2,1,0:T(8,128)(2,1)S(1)}, bf16[16,256,128]{2,1,0:T(8,128)(2,1)}, u32[]{:S(2)}) copy-start(bf16[16,256,128]{2,1,0:T(8,128)(2,1)} %param.21) | copy-start | bytes 3145732
  522.7 2.2 copy-start.17
